TPU v7x, 256 devices: a whole 4x4x8 slice. The times are simulated.
256 devices in a mesh: curve: 32 (over z, y), group: 8 (over x, core).
Axes of the slice: x: 4, y: 4, z: 8, core: 2. Of those that a mesh axis runs over, the one named last changes fastest.
Arguments:
- state: float32 [2560, 20, 16, 256], P(('curve', 'group')), may hold values from -6 to 6
- coarse_state: float32 [2560, 20, 640], P(('curve', 'group')), may hold values from -6 to 6
- coarse_kappa: float32 [2560, 20, 640], P(('curve', 'group')), may hold values from 0.03 to 0.16
- bound_shift: int32 [8, 32], P('group'), may hold values from -5 to 5, as said below
Outputs:
- new_state: float32 [5120, 20, 16, 256], P(('curve', 'group'))
Inputs may be any that keep to these rules, and one draw needn't show every extreme that they name: The last entry of every row is 0. In every row some device c with 1 <= c <= 32 - 2 has bound_shift[g, c - 1] = -5 and bound_shift[g, c] = 5, so it holds 20 patches after the regrid.
All inputs are finite; a program needn't handle non-finite values.
Results may differ from a plain program's by a relative error of at most 0.000094.
Values sent between devices are 32-bit elements; how exact they have to be, the bound alone decides.
A program may use at most 128 MiB of HBM per device.

v0:
```python
import jax
import jax.numpy as jnp
from jax import lax
from jax.sharding import PartitionSpec as P


def padded(block, sides, width):
    for axis, dim in sides:
        count = lax.axis_size(axis)
        forward = [(i, i + 1) for i in range(count - 1)]
        forward.append((count - 1, 0))
        backward = [(target, source) for source, target in forward]
        low = lax.ppermute(
            lax.slice_in_dim(block, block.shape[dim] - width, None, axis=dim), axis, forward
        )
        high = lax.ppermute(lax.slice_in_dim(block, 0, width, axis=dim), axis, backward)
        block = jnp.concatenate([low, block, high], axis=dim)
    return block


def shifted(block, axis, distance):
    devices = range(lax.axis_size(axis))
    route = [(i - distance, i) for i in devices if i - distance in devices]
    return lax.ppermute(block, axis, route)


def lane_tables(edge_cells, half_edge):
    lane_ids = jnp.arange(edge_cells * edge_cells, dtype=jnp.int32)
    lane_row = lane_ids // edge_cells
    lane_col = lane_ids % edge_cells
    source_ids = jnp.arange(half_edge * half_edge, dtype=jnp.int32)
    coarse_ids = jnp.arange(half_edge, dtype=jnp.int32)[:, None]
    inner_table = (
        (source_ids[:, None] // half_edge == lane_row[None, :] // 2)
        & (source_ids[:, None] % half_edge == lane_col[None, :] // 2)
    ).astype(jnp.float32)
    low_y = ((lane_row[None, :] == 0) & (coarse_ids == lane_col[None, :] // 2)).astype(jnp.float32)
    high_y = (
        (lane_row[None, :] == edge_cells - 1) & (coarse_ids == lane_col[None, :] // 2)
    ).astype(jnp.float32)
    low_z = ((lane_col[None, :] == 0) & (coarse_ids == lane_row[None, :] // 2)).astype(jnp.float32)
    high_z = (
        (lane_col[None, :] == edge_cells - 1) & (coarse_ids == lane_row[None, :] // 2)
    ).astype(jnp.float32)
    return (inner_table, low_y, high_y, low_z, high_z)


def spread(block, table):
    species, count_x, width = block.shape
    lanes = jnp.dot(
        block.reshape(species * count_x, width),
        table,
        precision=lax.Precision.HIGHEST,
        preferred_element_type=jnp.float32,
    )
    return lanes.reshape(species, count_x, table.shape[1])


def double_x(values):
    return jnp.repeat(values, 2, axis=1)


def neighbours(values, faces, edge_cells):
    x_lower, x_upper, y_lower, y_upper, z_lower, z_upper = faces
    lane_ids = jnp.arange(values.shape[2], dtype=jnp.int32)
    lane_row = lane_ids // edge_cells
    lane_col = lane_ids % edge_cells
    lower_x = jnp.concatenate([x_lower, values[:, :-1]], axis=1)
    upper_x = jnp.concatenate([values[:, 1:], x_upper], axis=1)
    lower_y = jnp.where(lane_row == 0, y_lower, jnp.roll(values, edge_cells, axis=2))
    upper_y = jnp.where(lane_row == edge_cells - 1, y_upper, jnp.roll(values, -edge_cells, axis=2))
    lower_z = jnp.where(lane_col == 0, z_lower, jnp.roll(values, 1, axis=2))
    upper_z = jnp.where(lane_col == edge_cells - 1, z_upper, jnp.roll(values, -1, axis=2))
    return (lower_x, upper_x, lower_y, upper_y, lower_z, upper_z)


def field_faces(block, sides, tables):
    inner_table, low_y, high_y, low_z, high_z = tables
    y_below, y_above, z_below, z_above = sides
    x_lower = spread(block[:, 0:1], inner_table)
    x_upper = spread(block[:, -1:], inner_table)
    y_lower = double_x(spread(y_below, low_y))
    y_upper = double_x(spread(y_above, high_y))
    z_lower = double_x(spread(z_below, low_z))
    z_upper = double_x(spread(z_above, high_z))
    return (x_lower, x_upper, y_lower, y_upper, z_lower, z_upper)


def smooth(patch_rows, outer_rows, species, edge_cells, coarse_x):
    half_edge = edge_cells // 2
    plane_size = half_edge * half_edge
    block_width = 2 * species * coarse_x * plane_size
    tables = lane_tables(edge_cells, half_edge)

    def one_patch(items):
        cells_row, outer_row = items
        patch_cells = cells_row.reshape(species, edge_cells, edge_cells * edge_cells)
        blocks = outer_row[:block_width].reshape(2, species, coarse_x, plane_size)
        sides = outer_row[block_width:].reshape(4, 2, species, half_edge, half_edge)
        state_sides = (sides[0, 0], sides[1, 0], sides[2, 0], sides[3, 0])
        kappa_sides = (sides[0, 1], sides[1, 1], sides[2, 1], sides[3, 1])
        kappa_fine = double_x(spread(blocks[1, :, 1:-1], tables[0]))
        near_cells = neighbours(
            patch_cells, field_faces(blocks[0], state_sides, tables), edge_cells
        )
        near_kappa = neighbours(kappa_fine, field_faces(blocks[1], kappa_sides, tables), edge_cells)
        change = jnp.zeros_like(patch_cells)
        for cell_value, kappa_value in zip(near_cells, near_kappa):
            change = change + 0.5 * (kappa_fine + kappa_value) * (cell_value - patch_cells)
        return patch_cells + change

    return lax.map(one_patch, (patch_rows, outer_rows))


def shards(state, coarse_state, coarse_kappa, bound_shift):
    patch_count, species, edge_cells, lane_count = state.shape
    half_count = patch_count // 2
    half_edge = edge_cells // 2
    coarse_x = half_edge + 2
    fields = jnp.stack([coarse_state, coarse_kappa], axis=1)
    blocks = fields.reshape(patch_count, 2, species, coarse_x, half_edge, half_edge)
    y_planes = jnp.stack([blocks[:, :, :, 1:-1, 0, :], blocks[:, :, :, 1:-1, half_edge - 1, :]])
    y_sides = padded(y_planes, (("group", 0),), 1)
    z_planes = jnp.stack(
        [blocks[:, :, :, 1:-1, :, 0], blocks[:, :, :, 1:-1, :, half_edge - 1]], axis=1
    )
    z_sides = padded(z_planes, (("curve", 0),), 1)
    side_rows = jnp.stack([y_sides[0], y_sides[3], z_sides[:-2, 1], z_sides[2:, 0]], axis=1)
    outer_rows = jnp.concatenate(
        [fields.reshape(patch_count, -1), side_rows.reshape(patch_count, -1)], axis=1
    )
    curve_here = lax.axis_index("curve")
    shift_row = bound_shift[0]
    shift_here = shift_row[curve_here]
    shift_before = jnp.where(curve_here > 0, shift_row[jnp.maximum(curve_here - 1, 0)], 0)
    slot_count = patch_count + shift_here - shift_before
    slot_index = jnp.arange(2 * patch_count, dtype=jnp.int32)
    slot_valid = slot_index < slot_count
    cell_width = species * edge_cells * lane_count
    packed = jnp.concatenate([state.reshape(patch_count, -1), outer_rows], axis=1)
    from_left = shifted(packed[patch_count - half_count :], "curve", 1)
    from_right = shifted(packed[:half_count], "curve", -1)
    window = jnp.concatenate([from_left, packed, from_right], axis=0)
    padded_rows = jnp.concatenate([window, jnp.zeros_like(packed)], axis=0)
    moved_rows = lax.dynamic_slice_in_dim(
        padded_rows, half_count + shift_before, 2 * patch_count, 0
    )
    moved_rows = jnp.where(slot_valid[:, None], moved_rows, 0.0)
    return smooth(
        moved_rows[:, :cell_width], moved_rows[:, cell_width:], species, edge_cells, coarse_x
    )


def solution(mesh):
    in_specs = (
        P(("curve", "group"), None, None, None),
        P(("curve", "group"), None, None),
        P(("curve", "group"), None, None),
        P("group", None),
    )
    out_specs = P(("curve", "group"), None, None, None)
    return jax.shard_map(shards, mesh=mesh, in_specs=in_specs, out_specs=out_specs, check_vma=False)
```

profile of v0, /device:TPU:1, one launch (start us, length us, event | category | flops | bytes accessed | tf_op | source)
XLA Modules:
  0.0 1055.5 jit_solution(5346399468818522978)
XLA Ops:
  0.0 2.0 copy.55
  2.0 3.2 copy.56
  5.2 4.1 pad_maximum_fusion.5
  10.2 2.1 collective-permute-start.2
  12.3 6.7 collective-permute-start.3
  20.3 2.1 collective-permute-start
  22.8 3.0 copy.70
  25.8 2.6 constant_dynamic-update-slice_fusion.2
  34.9 5.7 copy.62
  40.6 12.1 %reshape.1015 = f32[10,10240]{1,0:T(8,128)S(1)} reshape(f32[10,4,2,20,8,8]{5,4,3,2,1,0:T(8,128)} %copy.62) | data formatting | bytes 819200 | tf_op jit(solution)/shard_map/reshape | solution.py:130
  53.6 7.9 fusion.117
  61.5 3.2 collective-permute-start.4
  68.3 73.9 %collective-permute-done.4 = f32[5,117760]{1,0:T(8,128)} collective-permute-done((f32[5,117760]{1,0:T(8,128)}, f32[5,117760]{1,0:T(8,128)}, u32[]{:S(2)}, u32[]{:S(2)}) %collective-permute-start.4) | collective-permute-done | bytes 2355232 | tf_op jit(solution)/shard_map/ppermute | solution.py:24
  142.3 5.8 collective-permute-done.5
  148.0 8.7 fusion.107
  156.7 3.6 slice.432
  160.3 2.1 slice.433
  162.4 893.1 %while.15 = (s32[]{:T(128)}, f32[20,20,16,256]{3,2,1,0:T(8,128)}, f32[20,81920]{1,0:T(8,128)}, f32[20,35840]{1,0:T(8,128)}, s32[256]{0:T(256)S(1)}, /*index=5*/s...) while((s32[]{:T(128)}, f32[20,20,16,256]{3,2,1,0:T(8,128)}, ...), condition=%wide.region_1.2_spmd.clone.clone.clone, body=%wide.region_0.1_spmd.clone.clone.clone.sunk | while | flops 83123200 | bytes 32614624 | solution.py:112
  164.7 2.0 constant_dynamic-slice_fusion.4
  202.8 4.2 fusion.177
  247.4 4.2 fusion.177
  254.0 2.0 constant_dynamic-slice_fusion.4
  292.1 4.2 fusion.177
  298.6 2.0 constant_dynamic-slice_fusion.4
  336.8 4.2 fusion.177
  343.3 2.0 constant_dynamic-slice_fusion.4
  381.4 4.2 fusion.177
  387.9 2.0 constant_dynamic-slice_fusion.4
  426.1 4.2 fusion.177
  470.7 4.2 fusion.177
  477.3 2.0 constant_dynamic-slice_fusion.4
  515.4 4.2 fusion.177
  560.0 4.2 fusion.177
  566.6 2.0 constant_dynamic-slice_fusion.4
  604.7 4.2 fusion.177
  649.4 4.2 fusion.177
  694.0 4.2 fusion.177
  700.6 2.0 constant_dynamic-slice_fusion.4
  738.7 4.2 fusion.177
  745.2 2.0 constant_dynamic-slice_fusion.4
  783.3 4.2 fusion.177
  789.9 2.0 constant_dynamic-slice_fusion.4
  828.0 4.2 fusion.177
  872.6 4.2 fusion.177
  917.3 4.2 fusion.177
  962.0 4.2 fusion.177
  1006.6 4.2 fusion.177
  1051.3 4.2 fusion.177
  (1352 shorter events, 794.9 us)
Async XLA Ops:
  5.2 13.8 %copy-start = (f32[10,20,640]{1,2,0:T(8,128)S(1)}, f32[10,20,640]{1,2,0:T(8,128)}, u32[]{:S(2)}) copy-start(f32[10,20,640]{1,2,0:T(8,128)} %copy.56) | copy-start | bytes 1536004
  9.4 10.9 %copy-start.2 = (f32[10,2,20,8,8,1]{2,5,4,3,0,1:T(1,128)}, f32[10,2,20,8,8,1]{2,5,4,3,0,1:T(1,128)S(1)}, u32[]{:S(2)}) copy-start(f32[10,2,20,8,8,1]{2,5,4,3,0,1:T(1,128)S(1)} %get-tuple-element.331) | copy-start | bytes 307204
  9.4 10.9 %copy-start.4 = (f32[10,2,20,8,8,1]{2,5,4,3,0,1:T(1,128)}, f32[10,2,20,8,8,1]{2,5,4,3,0,1:T(1,128)S(1)}, u32[]{:S(2)}) copy-start(f32[10,2,20,8,8,1]{2,5,4,3,0,1:T(1,128)S(1)} %get-tuple-element.332) | copy-start | bytes 307204
  10.2 22.3 %collective-permute-start.2 = (f32[1,2,2,20,8,8]{3,5,4,0,2,1:T(8,128)}, f32[1,2,2,20,8,8]{3,5,4,0,2,1:T(8,128)S(1)}, u32[]{:S(2)}, u32[]{:S(2)}) collective-permute-start(f32[1,2,2,20,8,8]{3,5,4,0,2,1:T(8,128)} %get-tuple-element.333), channel_id=1, source_target_pairs={{0,8},{8,16},{16,24},{24,32},{32,40},{40,48},{48,56},{56,64},{64,7... | collective-permute-start | bytes 61448 | tf_op jit(solution)/shard_map/ppermute | solution.py:13
  12.3 10.0 copy-start.5
  12.3 20.2 %collective-permute-start.3 = (f32[1,2,2,20,8,8]{3,5,4,0,2,1:T(8,128)}, f32[1,2,2,20,8,8]{3,5,4,0,2,1:T(8,128)S(1)}, u32[]{:S(2)}, u32[]{:S(2)}) collective-permute-start(f32[1,2,2,20,8,8]{3,5,4,0,2,1:T(8,128)} %get-tuple-element.334), channel_id=1, source_target_pairs={{8,0},{16,8},{24,16},{32,24},{40,32},{48,40},{56,48},{64,56},{72,6... | collective-permute-start | bytes 61448 | tf_op jit(solution)/shard_map/ppermute | solution.py:16
  20.3 12.2 %collective-permute-start = (f32[1,10,2,20,8,8]{3,5,4,1,2,0:T(8,128)}, f32[1,10,2,20,8,8]{3,5,4,1,2,0:T(8,128)S(1)}, u32[]{:S(2)}, u32[]{:S(2)}) collective-permute-start(f32[1,10,2,20,8,8]{3,5,4,1,2,0:T(8,128)} %get-tuple-element.329), channel_id=1, source_target_pairs={{0,1},{1,2},{2,3},{3,4},{4,5},{5,6},{6,7},{7,0},{8,9},{9,10},{10,1... | collective-permute-start | bytes 307208 | tf_op jit(solution)/shard_map/ppermute | solution.py:13
  22.3 10.3 collective-permute-start.1
  25.8 2.7 copy-start.6
  25.8 2.7 copy-start.7
  28.6 4.8 copy-start.3
  32.5 0.8 copy-start.8
  53.6 12.7 %copy-start.9 = (s32[1,32]{1,0:T(1,128)S(1)}, s32[1,32]{1,0:T(1,128)}, u32[]{:S(2)}) copy-start(s32[1,32]{1,0:T(1,128)} %param.9) | copy-start | bytes 388
  61.5 80.7 %collective-permute-start.4 = (f32[5,117760]{1,0:T(8,128)}, f32[5,117760]{1,0:T(8,128)}, u32[]{:S(2)}, u32[]{:S(2)}) collective-permute-start(f32[5,117760]{1,0:T(8,128)} %get-tuple-element.328), channel_id=1, source_target_pairs={{0,8},{8,16},{16,24},{24,32},{32,40},{40,48},{48,56},{56,64},{64,7... | collective-permute-start | bytes 7065608 | tf_op jit(solution)/shard_map/ppermute | solution.py:24
  64.8 83.3 %collective-permute-start.5 = (f32[5,117760]{1,0:T(8,128)}, f32[5,117760]{1,0:T(8,128)}, u32[]{:S(2)}, u32[]{:S(2)}) collective-permute-start(f32[5,117760]{1,0:T(8,128)} %get-tuple-element.327), channel_id=1, source_target_pairs={{8,0},{16,8},{24,16},{32,24},{40,32},{48,40},{56,48},{64,56},{72,6... | collective-permute-start | bytes 7065608 | tf_op jit(solution)/shard_map/ppermute | solution.py:24
  191.7 11.0 %copy-start.1 = (f32[1,20,16,16]{3,2,1,0:T(8,128)S(1)}, f32[1,20,16,16]{3,2,1,0:T(8,128)}, u32[]{:S(2)}) copy-start(f32[1,20,16,16]{3,2,1,0:T(8,128)} %get-tuple-element.464) | copy-start | bytes 61444 | tf_op jit(solution)/shard_map/while
  236.4 11.1 %copy-start.1 = (f32[1,20,16,16]{3,2,1,0:T(8,128)S(1)}, f32[1,20,16,16]{3,2,1,0:T(8,128)}, u32[]{:S(2)}) copy-start(f32[1,20,16,16]{3,2,1,0:T(8,128)} %get-tuple-element.464) | copy-start | bytes 61444 | tf_op jit(solution)/shard_map/while
  281.1 11.0 %copy-start.1 = (f32[1,20,16,16]{3,2,1,0:T(8,128)S(1)}, f32[1,20,16,16]{3,2,1,0:T(8,128)}, u32[]{:S(2)}) copy-start(f32[1,20,16,16]{3,2,1,0:T(8,128)} %get-tuple-element.464) | copy-start | bytes 61444 | tf_op jit(solution)/shard_map/while
  325.7 11.0 %copy-start.1 = (f32[1,20,16,16]{3,2,1,0:T(8,128)S(1)}, f32[1,20,16,16]{3,2,1,0:T(8,128)}, u32[]{:S(2)}) copy-start(f32[1,20,16,16]{3,2,1,0:T(8,128)} %get-tuple-element.464) | copy-start | bytes 61444 | tf_op jit(solution)/shard_map/while
  370.4 11.1 %copy-start.1 = (f32[1,20,16,16]{3,2,1,0:T(8,128)S(1)}, f32[1,20,16,16]{3,2,1,0:T(8,128)}, u32[]{:S(2)}) copy-start(f32[1,20,16,16]{3,2,1,0:T(8,128)} %get-tuple-element.464) | copy-start | bytes 61444 | tf_op jit(solution)/shard_map/while
  415.0 11.0 %copy-start.1 = (f32[1,20,16,16]{3,2,1,0:T(8,128)S(1)}, f32[1,20,16,16]{3,2,1,0:T(8,128)}, u32[]{:S(2)}) copy-start(f32[1,20,16,16]{3,2,1,0:T(8,128)} %get-tuple-element.464) | copy-start | bytes 61444 | tf_op jit(solution)/shard_map/while
  459.7 11.0 %copy-start.1 = (f32[1,20,16,16]{3,2,1,0:T(8,128)S(1)}, f32[1,20,16,16]{3,2,1,0:T(8,128)}, u32[]{:S(2)}) copy-start(f32[1,20,16,16]{3,2,1,0:T(8,128)} %get-tuple-element.464) | copy-start | bytes 61444 | tf_op jit(solution)/shard_map/while
  504.3 11.1 %copy-start.1 = (f32[1,20,16,16]{3,2,1,0:T(8,128)S(1)}, f32[1,20,16,16]{3,2,1,0:T(8,128)}, u32[]{:S(2)}) copy-start(f32[1,20,16,16]{3,2,1,0:T(8,128)} %get-tuple-element.464) | copy-start | bytes 61444 | tf_op jit(solution)/shard_map/while
  549.0 11.0 %copy-start.1 = (f32[1,20,16,16]{3,2,1,0:T(8,128)S(1)}, f32[1,20,16,16]{3,2,1,0:T(8,128)}, u32[]{:S(2)}) copy-start(f32[1,20,16,16]{3,2,1,0:T(8,128)} %get-tuple-element.464) | copy-start | bytes 61444 | tf_op jit(solution)/shard_map/while
  593.6 11.0 %copy-start.1 = (f32[1,20,16,16]{3,2,1,0:T(8,128)S(1)}, f32[1,20,16,16]{3,2,1,0:T(8,128)}, u32[]{:S(2)}) copy-start(f32[1,20,16,16]{3,2,1,0:T(8,128)} %get-tuple-element.464) | copy-start | bytes 61444 | tf_op jit(solution)/shard_map/while
  638.3 11.1 %copy-start.1 = (f32[1,20,16,16]{3,2,1,0:T(8,128)S(1)}, f32[1,20,16,16]{3,2,1,0:T(8,128)}, u32[]{:S(2)}) copy-start(f32[1,20,16,16]{3,2,1,0:T(8,128)} %get-tuple-element.464) | copy-start | bytes 61444 | tf_op jit(solution)/shard_map/while
  683.0 11.0 %copy-start.1 = (f32[1,20,16,16]{3,2,1,0:T(8,128)S(1)}, f32[1,20,16,16]{3,2,1,0:T(8,128)}, u32[]{:S(2)}) copy-start(f32[1,20,16,16]{3,2,1,0:T(8,128)} %get-tuple-element.464) | copy-start | bytes 61444 | tf_op jit(solution)/shard_map/while
  727.6 11.0 %copy-start.1 = (f32[1,20,16,16]{3,2,1,0:T(8,128)S(1)}, f32[1,20,16,16]{3,2,1,0:T(8,128)}, u32[]{:S(2)}) copy-start(f32[1,20,16,16]{3,2,1,0:T(8,128)} %get-tuple-element.464) | copy-start | bytes 61444 | tf_op jit(solution)/shard_map/while
  772.3 11.1 %copy-start.1 = (f32[1,20,16,16]{3,2,1,0:T(8,128)S(1)}, f32[1,20,16,16]{3,2,1,0:T(8,128)}, u32[]{:S(2)}) copy-start(f32[1,20,16,16]{3,2,1,0:T(8,128)} %get-tuple-element.464) | copy-start | bytes 61444 | tf_op jit(solution)/shard_map/while
  816.9 11.0 %copy-start.1 = (f32[1,20,16,16]{3,2,1,0:T(8,128)S(1)}, f32[1,20,16,16]{3,2,1,0:T(8,128)}, u32[]{:S(2)}) copy-start(f32[1,20,16,16]{3,2,1,0:T(8,128)} %get-tuple-element.464) | copy-start | bytes 61444 | tf_op jit(solution)/shard_map/while
  861.6 11.0 %copy-start.1 = (f32[1,20,16,16]{3,2,1,0:T(8,128)S(1)}, f32[1,20,16,16]{3,2,1,0:T(8,128)}, u32[]{:S(2)}) copy-start(f32[1,20,16,16]{3,2,1,0:T(8,128)} %get-tuple-element.464) | copy-start | bytes 61444 | tf_op jit(solution)/shard_map/while
  906.2 11.1 %copy-start.1 = (f32[1,20,16,16]{3,2,1,0:T(8,128)S(1)}, f32[1,20,16,16]{3,2,1,0:T(8,128)}, u32[]{:S(2)}) copy-start(f32[1,20,16,16]{3,2,1,0:T(8,128)} %get-tuple-element.464) | copy-start | bytes 61444 | tf_op jit(solution)/shard_map/while
  950.9 11.0 %copy-start.1 = (f32[1,20,16,16]{3,2,1,0:T(8,128)S(1)}, f32[1,20,16,16]{3,2,1,0:T(8,128)}, u32[]{:S(2)}) copy-start(f32[1,20,16,16]{3,2,1,0:T(8,128)} %get-tuple-element.464) | copy-start | bytes 61444 | tf_op jit(solution)/shard_map/while
  995.6 11.0 %copy-start.1 = (f32[1,20,16,16]{3,2,1,0:T(8,128)S(1)}, f32[1,20,16,16]{3,2,1,0:T(8,128)}, u32[]{:S(2)}) copy-start(f32[1,20,16,16]{3,2,1,0:T(8,128)} %get-tuple-element.464) | copy-start | bytes 61444 | tf_op jit(solution)/shard_map/while
  1040.2 11.1 %copy-start.1 = (f32[1,20,16,16]{3,2,1,0:T(8,128)S(1)}, f32[1,20,16,16]{3,2,1,0:T(8,128)}, u32[]{:S(2)}) copy-start(f32[1,20,16,16]{3,2,1,0:T(8,128)} %get-tuple-element.464) | copy-start | bytes 61444 | tf_op jit(solution)/shard_map/while
where the time goes:
time: 1070 us; the launch traced here: 1060 us
  local copies, waits for them, and re-layouts  782 us (73%)
  other arithmetic  102 us (10%)
  waiting for transfers between devices  79.8 us (7%)
  matrix products  69 us (6%)
  starting transfers between devices  15.6 us (1%)
    reshape x200, local copies, waits for them, and re-layouts, double_x(): return jnp.repeat(values, 2, axis=1)  298 us
    broadcast_in_dim x180, local copies, waits for them, and re-layouts, double_x(): return jnp.repeat(values, 2, axis=1)  133 us
    dynamic_update_slice x20, other arithmetic, smooth(): return lax.map(one_patch, (patch_rows, outer_rows))  84.8 us
    ppermute x2, waiting for transfers between devices, shifted(): return lax.ppermute(block, axis, route)  79.7 us
    dot_general x260, matrix products, spread(): jnp.dot(block.reshape(species * count_x, width), table, precision=lax.Pre...  69 us
    concatenate x60, local copies, waits for them, and re-layouts, neighbours(): jnp.roll(values, -1, axis=2)  48.5 us
    concatenate x40, local copies, waits for them, and re-layouts, neighbours(): jnp.roll(values, -edge_cells, axis=2)  39.8 us
    dynamic_slice x20, local copies, waits for them, and re-layouts, smooth(): return lax.map(one_patch, (patch_rows, outer_rows))  39.5 us
  transfers between devices with their start and end apart: 6, of which 3 were waited for; matrix products, arithmetic and copies ran while one was open for 1% of the time, Pallas kernels for 0%

commit v1 on v0

v1 whole, which is shorter than its diff:
```python
import jax
import jax.numpy as jnp
import numpy as np
from jax import lax
from jax.experimental import pallas as pl
from jax.experimental.pallas import tpu as pltpu
from jax.sharding import PartitionSpec as P

MESH = pl.DeviceIdType.MESH
SPEC = 20
EDGE = 16
LANES = EDGE * EDGE
PATCHES = 10
HALF = 5
COARSE = 640
PITCH = 24
TILES = COARSE // 128
DEPTH = 256
CHUNK = 10
ROWS = CHUNK * EDGE
CHUNKS = SPEC // CHUNK
BLOCK = 2


def row_tables():
    own = np.zeros((SPEC * EDGE, DEPTH), np.float32)
    outer = np.zeros_like(own)
    face = np.zeros_like(own)
    for s in range(SPEC):
        for i in range(EDGE):
            half = i // 2
            own[s * EDGE + i, (half + 1) * PITCH + s] = 1.0
            outer[s * EDGE + i, (half + 2 if i % 2 else half) * PITCH + s] = 1.0
            if i == 0:
                face[s * EDGE + i, s] = 1.0
            if i == EDGE - 1:
                face[s * EDGE + i, 9 * PITCH + s] = 1.0
    return np.stack([own, outer, face])


def lane_tables():
    half = np.zeros((64, LANES), np.float32)
    y_own, y_side, y_face = np.zeros_like(half), np.zeros_like(half), np.zeros_like(half)
    z_own, z_side, z_face = np.zeros_like(half), np.zeros_like(half), np.zeros_like(half)
    for r in range(EDGE):
        for q in range(EDGE):
            lane, cy, cz = r * EDGE + q, r // 2, q // 2
            here = cy * 8 + cz
            half[here, lane] = 0.5
            y_own[here, lane] += 0.5
            z_own[here, lane] += 0.5
            near = r + 1 if r % 2 else r - 1
            if near < 0:
                y_side[56 + cz, lane], y_face[56 + cz, lane] = 0.5, 1.0
            elif near >= EDGE:
                y_side[cz, lane], y_face[cz, lane] = 0.5, 1.0
            else:
                y_own[near // 2 * 8 + cz, lane] += 0.5
            near = q + 1 if q % 2 else q - 1
            if near < 0:
                z_side[cy * 8 + 7, lane], z_face[cy * 8 + 7, lane] = 0.5, 1.0
            elif near >= EDGE:
                z_side[cy * 8, lane], z_face[cy * 8, lane] = 0.5, 1.0
            else:
                z_own[cy * 8 + near // 2, lane] += 0.5
    parts = [half, y_side, y_own, z_own, z_side, y_face, z_face, 2.0 * half]
    return np.concatenate([np.concatenate([part, part]) for part in parts])


def lane_iota(rows):
    return lax.broadcasted_iota(jnp.int32, (rows, 128), 1)


def stage_tile(tile, values, target, pick):
    lane = lane_iota(SPEC)
    high = values.astype(jnp.bfloat16).astype(jnp.float32)
    rest = values - high
    even = jnp.where(lane < 64, high, pltpu.roll(rest, 64, 1))
    odd = jnp.where(lane < 64, pltpu.roll(high, 64, 1), rest)
    target[pick, 2 * tile * PITCH : 2 * tile * PITCH + SPEC, :] = even
    target[pick, (2 * tile + 1) * PITCH : (2 * tile + 1) * PITCH + SPEC, :] = odd


def exchange_kernel(
    state_ref,
    coarse_state_ref,
    coarse_kappa_ref,
    rows_ref,
    lanes_ref,
    own_ref,
    left_ref,
    right_ref,
    cells,
    coarse,
    row_mats,
    lane_mats,
    staged,
    sides,
    pack_out,
    pack_in,
    edge_out,
    edge_in,
    weights,
    cell_sem,
    coarse_sem,
    table_sem,
    pack_send,
    pack_recv,
    edge_send,
    edge_recv,
    move_send,
    move_recv,
):
    curve = lax.axis_index("curve")
    group = lax.axis_index("group")
    n_curve = lax.axis_size("curve")
    n_group = lax.axis_size("group")
    ahead = (lax.rem(curve + 1, n_curve), group)
    behind = (lax.rem(curve + n_curve - 1, n_curve), group)
    above = (curve, lax.rem(group + 1, n_group))
    below = (curve, lax.rem(group + n_group - 1, n_group))

    def load_coarse(field, part, begin, count):
        source = (coarse_state_ref, coarse_kappa_ref)[field]
        return pltpu.make_async_copy(
            source.at[pl.ds(begin, count)],
            coarse.at[field, pl.ds(begin + 1, count)],
            coarse_sem.at[field, part],
        )

    def load_cells(patch):
        return pltpu.make_async_copy(state_ref.at[patch], cells.at[patch], cell_sem.at[patch])

    def load_tables():
        return (
            pltpu.make_async_copy(rows_ref, row_mats, table_sem.at[0]),
            pltpu.make_async_copy(lanes_ref, lane_mats, table_sem.at[1]),
        )

    parts = ((3, 4), (0, 3), (7, 3))
    for field in range(2):
        load_coarse(field, 0, *parts[0]).start()
    for copy in load_tables():
        copy.start()
    for patch in (5, 4):
        load_cells(patch).start()
    for part in (1, 2):
        for field in range(2):
            load_coarse(field, part, *parts[part]).start()
    for patch in (6, 3, 7, 2, 8, 1, 9, 0):
        load_cells(patch).start()

    barrier = pltpu.get_barrier_semaphore()
    for device in (above, below, ahead, behind):
        pl.semaphore_signal(barrier, inc=1, device_id=device, device_id_type=MESH)

    staged[...] = jnp.zeros_like(staged)
    sides[...] = jnp.zeros_like(sides)

    lane = lane_iota(SPEC)
    row_of = (lane % 64) // 8

    def pack(slot, patches, first):
        for tile in range(TILES):
            up = jnp.zeros((SPEC, 128), jnp.float32)
            down = jnp.zeros((SPEC, 128), jnp.float32)
            for place, patch in enumerate(patches):
                for field in range(2):
                    j = (first + place) * 2 + field
                    values = coarse[field, patch + 1, :, tile * 128 : (tile + 1) * 128]
                    up = jnp.where(row_of == 7 - j, pltpu.roll(values, (128 - 8 * j) % 128, 1), up)
                    down = jnp.where(row_of == j, pltpu.roll(values, 8 * j, 1), down)
            pack_out[0, slot, :, tile * 128 : (tile + 1) * 128] = up
            pack_out[1, slot, :, tile * 128 : (tile + 1) * 128] = down

    def pack_copy(way, slot):
        return pltpu.make_async_remote_copy(
            src_ref=pack_out.at[way, slot],
            dst_ref=pack_in.at[way, slot],
            send_sem=pack_send.at[way, slot],
            recv_sem=pack_recv.at[way, slot],
            device_id=(above, below)[way],
            device_id_type=MESH,
        )

    def edge_copy(way):
        return pltpu.make_async_remote_copy(
            src_ref=edge_out.at[way],
            dst_ref=edge_in.at[way],
            send_sem=edge_send.at[way],
            recv_sem=edge_recv.at[way],
            device_id=(ahead, behind)[way],
            device_id_type=MESH,
        )

    def move_copy(way, k, chunk):
        patch = 5 + k if way == 0 else 4 - k
        slot = k if way == 0 else 4 - k
        part = pl.ds(chunk * CHUNK, CHUNK)
        return pltpu.make_async_remote_copy(
            src_ref=own_ref.at[patch, part],
            dst_ref=(left_ref, right_ref)[way].at[slot, part],
            send_sem=move_send.at[way, k, chunk],
            recv_sem=move_recv.at[way, k, chunk],
            device_id=(ahead, behind)[way],
            device_id_type=MESH,
        )

    def stage(slot):
        for field in range(2):
            for tile in range(TILES):
                values = coarse[field, slot, :, tile * 128 : (tile + 1) * 128]
                stage_tile(tile, values, staged.at[field], slot)

    for field in range(2):
        load_coarse(field, 0, *parts[0]).wait()
    pack(0, (5, 4), 2)
    pl.semaphore_wait(barrier, 4)
    for way in range(2):
        pack_copy(way, 0).start()
    stage(5)
    stage(6)
    for copy in load_tables():
        copy.wait()

    def smooth_chunk(patch, chunk, factors, kappa_own, state_own):
        begin = pl.multiple_of(chunk * ROWS, ROWS)
        rows = [row_mats[t, pl.ds(begin, ROWS), :] for t in range(3)]

        def table(first, count):
            return lane_mats[first * 128 : (first + count) * 128, :]

        def dot(a, b):
            return jnp.dot(a, b, preferred_element_type=jnp.float32)

        spread = dot(rows[0], factors).astype(jnp.bfloat16)
        outer = dot(rows[1], kappa_own).astype(jnp.bfloat16)
        face = dot(rows[2], state_own).astype(jnp.bfloat16)
        weights[0] = dot(spread[:, 128:256], table(0, 1))
        weights[1] = dot(outer, table(0, 1))
        weights[2] = dot(spread[:, 0:256], table(1, 2))
        weights[3] = dot(spread[:, 128:384], table(3, 2))
        weights[4] = dot(spread[:, 384:512], table(5, 1))
        weights[5] = dot(spread[:, 512:640], table(6, 1))
        weights[6] = dot(face, table(7, 1))

        shape = (BLOCK, EDGE, LANES)
        x = lax.broadcasted_iota(jnp.int32, shape, 1)
        lanes = lax.broadcasted_iota(jnp.int32, shape, 2)
        y, z = lanes // EDGE, lanes % EDGE

        def block(b, carry):
            species = chunk * CHUNK + b * BLOCK
            p = cells[patch, pl.ds(species, BLOCK)]
            at = pl.ds(pl.multiple_of(b * BLOCK * EDGE, BLOCK * EDGE), BLOCK * EDGE)
            half, half_outer, w_y, w_z, u_y, u_z, u_x = (
                weights[t, at, :].reshape(shape) for t in range(7)
            )

            def pair(index, axis, step, extent, outside):
                up = pltpu.roll(p, extent - step, axis)
                down = pltpu.roll(p, step, axis)
                odd = index % 2 == 1
                inner = jnp.where(odd, down, up)
                far = jnp.where(odd, up, down)
                far = jnp.where((index == 0) | (index == EDGE - 1), outside, far)
                return inner, far

            in_x, out_x = pair(x, 1, 1, EDGE, u_x)
            in_y, out_y = pair(y, 2, EDGE, LANES, u_y)
            in_z, out_z = pair(z, 2, 1, LANES, u_z)
            change = half * (2.0 * (in_x + in_y + in_z) - 6.0 * p)
            change = change + (half + half_outer) * (out_x - p)
            change = change + w_y * (out_y - p)
            change = change + w_z * (out_z - p)
            own_ref[patch, pl.ds(species, BLOCK)] = p + change
            return carry

        lax.fori_loop(0, CHUNK // BLOCK, block, 0)

    def smooth(way, k):
        patch = 5 + k if way == 0 else 4 - k
        slot = (k + 1) // 2
        base = 2 * lax.rem(k + 1, 2) + way
        for field in range(2):
            j = base * 2 + field
            back = 8 * j
            forth = lax.rem(128 - 8 * j, 128)
            for tile in range(TILES):
                part = slice(tile * 128, (tile + 1) * 128)
                low = pltpu.roll(pack_in[0, slot, :, part], back, 1)
                high = pltpu.roll(pack_in[1, slot, :, part], forth, 1)
                values = jnp.where(row_of == 7, low, jnp.where(row_of == 0, high, 0.0))
                stage_tile(tile, values, sides, field)
        z = lane_iota(DEPTH) % 8

        def across(field):
            low, high = staged[field, patch], staged[field, patch + 2]
            return jnp.where(z == 7, low, jnp.where(z == 0, high, 0.0)).astype(jnp.bfloat16)

        state_own = staged[0, patch + 1].astype(jnp.bfloat16)
        kappa_own = staged[1, patch + 1].astype(jnp.bfloat16)
        factors = jnp.concatenate(
            [
                sides[1].astype(jnp.bfloat16),
                kappa_own,
                across(1),
                sides[0].astype(jnp.bfloat16),
                across(0),
            ],
            axis=1,
        )
        load_cells(patch).wait()
        for chunk in range(CHUNKS):
            smooth_chunk(patch, chunk, factors, kappa_own, state_own)
            move_copy(way, k, chunk).start()

    def step(k, carry):
        @pl.when(k == 0)
        def _():
            for way in range(2):
                pack_copy(way, 0).wait_recv()

        @pl.when(k == 1)
        def _():
            for way in range(2):
                pack_copy(way, 1).wait_recv()

        @pl.when(k == 3)
        def _():
            for way in range(2):
                pack_copy(way, 2).wait_recv()

        @pl.when(k == 4)
        def _():
            for way in range(2):
                edge_copy(way).wait_recv()
            for field in range(2):
                for tile in range(TILES):
                    part = slice(tile * 128, (tile + 1) * 128)
                    low = pltpu.roll(edge_in[0, field], (7 - tile) % 128, 1)
                    high = pltpu.roll(edge_in[1, field], (128 - tile) % 128, 1)
                    coarse[field, 0, :, part] = low
                    coarse[field, 11, :, part] = high

        stage(7 + k)
        stage(4 - k)
        smooth(0, k)
        smooth(1, k)

        @pl.when(k == 0)
        def _():
            for part in (1, 2):
                for field in range(2):
                    load_coarse(field, part, *parts[part]).wait()
            pack(1, (6, 3, 7, 2), 0)
            pack(2, (8, 1, 9, 0), 0)
            for field in range(2):
                up = jnp.zeros((SPEC, 128), jnp.float32)
                down = jnp.zeros((SPEC, 128), jnp.float32)
                for tile in range(TILES):
                    part = slice(tile * 128, (tile + 1) * 128)
                    last = coarse[field, PATCHES, :, part]
                    first = coarse[field, 1, :, part]
                    up = jnp.where(lane % 8 == tile, pltpu.roll(last, (128 + tile - 7) % 128, 1), up)
                    down = jnp.where(lane % 8 == tile, pltpu.roll(first, tile, 1), down)
                edge_out[0, field] = up
                edge_out[1, field] = down
            for way in range(2):
                pack_copy(way, 1).start()
                pack_copy(way, 2).start()
                edge_copy(way).start()

        return carry

    lax.fori_loop(0, HALF, step, 0)

    for way in range(2):
        for slot in range(3):
            pack_copy(way, slot).wait_send()
        edge_copy(way).wait_send()
        for k in range(HALF):
            for chunk in range(CHUNKS):
                move_copy(way, k, chunk).wait()


def place_kernel(shift_ref, own_ref, left_ref, right_ref, out_ref, zeros, sem):
    curve = lax.axis_index("curve")
    here = shift_ref[0, curve]
    before = jnp.where(curve > 0, shift_ref[0, jnp.maximum(curve - 1, 0)], 0)
    count = PATCHES + here - before
    zeros[...] = jnp.zeros_like(zeros)
    for slot in range(2 * PATCHES):
        position = before + slot
        used = slot < count
        target = out_ref.at[slot]

        def put(source):
            pltpu.make_async_copy(source, target, sem).start()

        @pl.when(used & (position < 0))
        def _():
            put(left_ref.at[jnp.clip(position + HALF, 0, HALF - 1)])

        @pl.when(used & (position >= PATCHES))
        def _():
            put(right_ref.at[jnp.clip(position - PATCHES, 0, HALF - 1)])

        @pl.when(used & (position >= 0) & (position < PATCHES))
        def _():
            put(own_ref.at[jnp.clip(position, 0, PATCHES - 1)])

        @pl.when(jnp.logical_not(used))
        def _():
            put(zeros)

    pltpu.make_async_copy(out_ref, out_ref, sem).wait()


def shards(state, coarse_state, coarse_kappa, bound_shift):
    f32, bf16 = jnp.float32, jnp.bfloat16
    patch = (SPEC, EDGE, LANES)
    hbm = pl.BlockSpec(memory_space=pltpu.HBM)
    vmem = pl.BlockSpec(memory_space=pltpu.VMEM)
    row_table = jnp.asarray(row_tables(), bf16)
    lane_table = jnp.asarray(lane_tables(), bf16)
    own, left, right = pl.pallas_call(
        exchange_kernel,
        name="exchange",
        out_shape=[
            jax.ShapeDtypeStruct((count,) + patch, f32) for count in (PATCHES, HALF, HALF)
        ],
        in_specs=[hbm] * 5,
        out_specs=[vmem] * 3,
        scratch_shapes=[
            pltpu.VMEM((PATCHES,) + patch, f32),
            pltpu.VMEM((2, PATCHES + 2, SPEC, COARSE), f32),
            pltpu.VMEM(row_table.shape, bf16),
            pltpu.VMEM(lane_table.shape, bf16),
            pltpu.VMEM((2, PATCHES + 2, DEPTH, 128), f32),
            pltpu.VMEM((2, DEPTH, 128), f32),
            pltpu.VMEM((2, 3, SPEC, COARSE), f32),
            pltpu.VMEM((2, 3, SPEC, COARSE), f32),
            pltpu.VMEM((2, 2, SPEC, 128), f32),
            pltpu.VMEM((2, 2, SPEC, 128), f32),
            pltpu.VMEM((7, ROWS, LANES), f32),
            pltpu.SemaphoreType.DMA((PATCHES,)),
            pltpu.SemaphoreType.DMA((2, 3)),
            pltpu.SemaphoreType.DMA((2,)),
            pltpu.SemaphoreType.DMA((2, 3)),
            pltpu.SemaphoreType.DMA((2, 3)),
            pltpu.SemaphoreType.DMA((2,)),
            pltpu.SemaphoreType.DMA((2,)),
            pltpu.SemaphoreType.DMA((2, HALF, CHUNKS)),
            pltpu.SemaphoreType.DMA((2, HALF, CHUNKS)),
        ],
        compiler_params=pltpu.CompilerParams(
            collective_id=0, has_side_effects=True, vmem_limit_bytes=36 << 20
        ),
        cost_estimate=pl.CostEstimate(flops=8 << 30, bytes_accessed=12 << 20, transcendentals=0),
    )(state, coarse_state, coarse_kappa, row_table, lane_table)
    return pl.pallas_call(
        place_kernel,
        name="place",
        out_shape=jax.ShapeDtypeStruct((2 * PATCHES,) + patch, f32),
        in_specs=[pl.BlockSpec(memory_space=pltpu.SMEM)] + [vmem] * 3,
        out_specs=hbm,
        scratch_shapes=[pltpu.VMEM(patch, f32), pltpu.SemaphoreType.DMA],
        compiler_params=pltpu.CompilerParams(vmem_limit_bytes=16 << 20),
        cost_estimate=pl.CostEstimate(flops=0, bytes_accessed=7 << 20, transcendentals=0),
    )(bound_shift, own, left, right)


def solution(mesh):
    in_specs = (
        P(("curve", "group"), None, None, None),
        P(("curve", "group"), None, None),
        P(("curve", "group"), None, None),
        P("group", None),
    )
    out_specs = P(("curve", "group"), None, None, None)
    return jax.shard_map(shards, mesh=mesh, in_specs=in_specs, out_specs=out_specs, check_vma=False)
```

time: 1070 us -> 67.1 us (0.06)
  the two profiles are of different devices: /device:TPU:1 before, /device:TPU:7 now
where the time goes in v1:
time: 67.1 us; the launch traced here: 66.8 us
  Pallas kernels  60.6 us (90%)
  local copies, waits for them, and re-layouts  6.16 us (9%)
    pallas_call x1, Pallas kernels, shards(): pl.pallas_call(exchange_kernel, name='exchange', out_shape=[jax.ShapeDtyp...  57.3 us
    unnamed x12, local copies, waits for them, and re-layouts  6.16 us
    pallas_call x1, Pallas kernels, shards(): pl.pallas_call(place_kernel, name='place', out_shape=jax.ShapeDtypeStruct...  3.29 us

profile of v1, /device:TPU:7, one launch (start us, length us, event | category | flops | bytes accessed | tf_op | source)
XLA Modules:
  0.0 66.8 jit_solution(6334452033062646111)
XLA Ops:
  0.0 0.0 copy-start
  0.0 0.0 copy-start.1
  0.0 1.9 %copy-done.1 = f32[10,20,16,256]{3,2,1,0:T(8,128)S(1)} copy-done((f32[10,20,16,256]{3,2,1,0:T(8,128)S(1)}, f32[10,20,16,256]{3,2,1,0:T(8,128)}, u32[]{:S(2)}) %copy-start.1) | copy-done | bytes 3276824
  1.9 0.0 copy-start.2
  1.9 1.1 %copy-done.2 = f32[10,20,640]{2,1,0:T(8,128)S(1)} copy-done((f32[10,20,640]{2,1,0:T(8,128)S(1)}, f32[10,20,640]{2,1,0:T(8,128)}, u32[]{:S(2)}) %copy-start.2) | copy-done | bytes 512024
  3.0 0.0 copy-start.3
  3.0 1.1 %copy-done.3 = f32[10,20,640]{2,1,0:T(8,128)S(1)} copy-done((f32[10,20,640]{2,1,0:T(8,128)S(1)}, f32[10,20,640]{2,1,0:T(8,128)}, u32[]{:S(2)}) %copy-start.3) | copy-done | bytes 512024
  4.1 0.0 copy-start.4
  4.1 1.0 %copy-done.4 = bf16[1024,256]{1,0:T(8,128)(2,1)S(1)} copy-done((bf16[1024,256]{1,0:T(8,128)(2,1)S(1)}, bf16[1024,256]{1,0:T(8,128)(2,1)}, u32[]{:S(2)}) %copy-start.4) | copy-done | bytes 524312
  5.1 0.0 copy-start.5
  5.1 1.0 %copy-done.5 = bf16[3,320,256]{2,1,0:T(8,128)(2,1)S(1)} copy-done((bf16[3,320,256]{2,1,0:T(8,128)(2,1)S(1)}, bf16[3,320,256]{2,1,0:T(8,128)(2,1)}, u32[]{:S(2)}) %copy-start.5) | copy-done | bytes 491544
  6.2 57.3 %exchange.1 = (f32[10,20,16,256]{3,2,1,0:T(8,128)S(1)}, f32[5,20,16,256]{3,2,1,0:T(8,128)S(1)}, f32[5,20,16,256]{3,2,1,0:T(8,128)S(1)}) custom-call(f32[10,20,16,256]{3,2,1,0:T(8,128)S(1)} %copy-done.1, f32[10,20,640]{2,1,0:T(8,128)S(1)} %copy-done.2, f32[10,20,640]{2,1,0:T(8,128)S(1)} %copy-done.3, bf16[3,320,256]{2,1,0:T(8,128)(2,1)S(1)} %copy-done.5, ...), custom_call_target="tpu_custom_call" | custom-call | flops 8589934592 | bytes 12582912 | tf_op jit(solution)/shard_map/exchange/pallas_call | solution.py:427
  63.5 0.0 copy-done
  63.5 3.3 %place.1 = f32[20,20,16,256]{3,2,1,0:T(8,128)} custom-call(s32[1,32]{1,0:T(1,128)S(1)} %copy-done, f32[10,20,16,256]{3,2,1,0:T(8,128)S(1)} %get-tuple-element.8.own_ref, f32[5,20,16,256]{3,2,1,0:T(8,128)S(1)} %get-tuple-element.9.left_ref, f32[5,20,16,256]{3,2,1,0:T(8,128)S(1)} %get-tuple-element.10.right_ref), custom_call_target="tpu_custom_call" | custom-call | bytes 7340032 | tf_op jit(solution)/shard_map/place/pallas_call | solution.py:462
Async XLA Ops:
  0.0 63.5 %copy-start = (s32[1,32]{1,0:T(1,128)S(1)}, s32[1,32]{1,0:T(1,128)}, u32[]{:S(2)}) copy-start(s32[1,32]{1,0:T(1,128)} %shift_ref.1) | copy-start | bytes 388
  0.0 1.9 %copy-start.1 = (f32[10,20,16,256]{3,2,1,0:T(8,128)S(1)}, f32[10,20,16,256]{3,2,1,0:T(8,128)}, u32[]{:S(2)}) copy-start(f32[10,20,16,256]{3,2,1,0:T(8,128)} %state_ref.1) | copy-start | bytes 9830404
  1.9 1.1 %copy-start.2 = (f32[10,20,640]{2,1,0:T(8,128)S(1)}, f32[10,20,640]{2,1,0:T(8,128)}, u32[]{:S(2)}) copy-start(f32[10,20,640]{2,1,0:T(8,128)} %coarse_state_ref.1) | copy-start | bytes 1536004
  3.0 1.1 %copy-start.3 = (f32[10,20,640]{2,1,0:T(8,128)S(1)}, f32[10,20,640]{2,1,0:T(8,128)}, u32[]{:S(2)}) copy-start(f32[10,20,640]{2,1,0:T(8,128)} %coarse_kappa_ref.1) | copy-start | bytes 1536004
  4.1 1.0 %copy-start.4 = (bf16[1024,256]{1,0:T(8,128)(2,1)S(1)}, bf16[1024,256]{1,0:T(8,128)(2,1)}, u32[]{:S(2)}) copy-start(bf16[1024,256]{1,0:T(8,128)(2,1)} %constant.5.clone.lanes_ref) | copy-start | bytes 1572868
  5.1 1.0 %copy-start.5 = (bf16[3,320,256]{2,1,0:T(8,128)(2,1)S(1)}, bf16[3,320,256]{2,1,0:T(8,128)(2,1)}, u32[]{:S(2)}) copy-start(bf16[3,320,256]{2,1,0:T(8,128)(2,1)} %constant.4.clone.rows_ref) | copy-start | bytes 1474564

commit v2 on v1

--- a/solution.py
+++ b/solution.py
@@ -15,27 +15,10 @@
 COARSE = 640
 PITCH = 24
 TILES = COARSE // 128
-DEPTH = 256
 CHUNK = 10
-ROWS = CHUNK * EDGE
 CHUNKS = SPEC // CHUNK
 BLOCK = 2
-
-
-def row_tables():
-    own = np.zeros((SPEC * EDGE, DEPTH), np.float32)
-    outer = np.zeros_like(own)
-    face = np.zeros_like(own)
-    for s in range(SPEC):
-        for i in range(EDGE):
-            half = i // 2
-            own[s * EDGE + i, (half + 1) * PITCH + s] = 1.0
-            outer[s * EDGE + i, (half + 2 if i % 2 else half) * PITCH + s] = 1.0
-            if i == 0:
-                face[s * EDGE + i, s] = 1.0
-            if i == EDGE - 1:
-                face[s * EDGE + i, 9 * PITCH + s] = 1.0
-    return np.stack([own, outer, face])
+FLAT = SPEC * 8
 
 
 def lane_tables():
@@ -63,7 +46,7 @@
                 z_side[cy * 8, lane], z_face[cy * 8, lane] = 0.5, 1.0
             else:
                 z_own[cy * 8 + near // 2, lane] += 0.5
-    parts = [half, y_side, y_own, z_own, z_side, y_face, z_face, 2.0 * half]
+    parts = [half, half, y_own, y_side, z_own, z_side, y_face, z_face, 2.0 * half]
     return np.concatenate([np.concatenate([part, part]) for part in parts])
 
 
@@ -71,36 +54,43 @@
     return lax.broadcasted_iota(jnp.int32, (rows, 128), 1)
 
 
-def stage_tile(tile, values, target, pick):
+def split_pair(values):
     lane = lane_iota(SPEC)
     high = values.astype(jnp.bfloat16).astype(jnp.float32)
     rest = values - high
     even = jnp.where(lane < 64, high, pltpu.roll(rest, 64, 1))
     odd = jnp.where(lane < 64, pltpu.roll(high, 64, 1), rest)
-    target[pick, 2 * tile * PITCH : 2 * tile * PITCH + SPEC, :] = even
-    target[pick, (2 * tile + 1) * PITCH : (2 * tile + 1) * PITCH + SPEC, :] = odd
+    return even, odd
+
+
+def put_rows(target, place, values):
+    if 0 <= place < 8:
+        target[pl.ds(place, SPEC, stride=8), :] = values
 
 
 def exchange_kernel(
     state_ref,
     coarse_state_ref,
     coarse_kappa_ref,
-    rows_ref,
     lanes_ref,
     own_ref,
     left_ref,
     right_ref,
     cells,
     coarse,
-    row_mats,
     lane_mats,
     staged,
+    outer,
     sides,
+    faces,
+    face_rows,
     pack_out,
     pack_in,
     edge_out,
     edge_in,
     weights,
+    fix_out,
+    fix_in,
     cell_sem,
     coarse_sem,
     table_sem,
@@ -110,6 +100,8 @@
     edge_recv,
     move_send,
     move_recv,
+    fix_send,
+    fix_recv,
 ):
     curve = lax.axis_index("curve")
     group = lax.axis_index("group")
@@ -131,17 +123,13 @@
     def load_cells(patch):
         return pltpu.make_async_copy(state_ref.at[patch], cells.at[patch], cell_sem.at[patch])
 
-    def load_tables():
-        return (
-            pltpu.make_async_copy(rows_ref, row_mats, table_sem.at[0]),
-            pltpu.make_async_copy(lanes_ref, lane_mats, table_sem.at[1]),
-        )
+    def load_table():
+        return pltpu.make_async_copy(lanes_ref, lane_mats, table_sem)
 
     parts = ((3, 4), (0, 3), (7, 3))
     for field in range(2):
         load_coarse(field, 0, *parts[0]).start()
-    for copy in load_tables():
-        copy.start()
+    load_table().start()
     for patch in (5, 4):
         load_cells(patch).start()
     for part in (1, 2):
@@ -154,8 +142,7 @@
     for device in (above, below, ahead, behind):
         pl.semaphore_signal(barrier, inc=1, device_id=device, device_id_type=MESH)
 
-    staged[...] = jnp.zeros_like(staged)
-    sides[...] = jnp.zeros_like(sides)
+    faces[...] = jnp.zeros_like(faces)
 
     lane = lane_iota(SPEC)
     row_of = (lane % 64) // 8
@@ -206,82 +193,165 @@
             device_id_type=MESH,
         )
 
+    def fix_copy(way):
+        return pltpu.make_async_remote_copy(
+            src_ref=fix_out.at[way],
+            dst_ref=fix_in.at[way],
+            send_sem=fix_send.at[way],
+            recv_sem=fix_recv.at[way],
+            device_id=(ahead, behind)[way],
+            device_id_type=MESH,
+        )
+
     def stage(slot):
         for field in range(2):
             for tile in range(TILES):
                 values = coarse[field, slot, :, tile * 128 : (tile + 1) * 128]
-                stage_tile(tile, values, staged.at[field], slot)
-
-    for field in range(2):
-        load_coarse(field, 0, *parts[0]).wait()
-    pack(0, (5, 4), 2)
-    pl.semaphore_wait(barrier, 4)
-    for way in range(2):
-        pack_copy(way, 0).start()
-    stage(5)
-    stage(6)
-    for copy in load_tables():
-        copy.wait()
-
-    def smooth_chunk(patch, chunk, factors, kappa_own, state_own):
-        begin = pl.multiple_of(chunk * ROWS, ROWS)
-        rows = [row_mats[t, pl.ds(begin, ROWS), :] for t in range(3)]
-
-        def table(first, count):
-            return lane_mats[first * 128 : (first + count) * 128, :]
-
-        def dot(a, b):
-            return jnp.dot(a, b, preferred_element_type=jnp.float32)
-
-        spread = dot(rows[0], factors).astype(jnp.bfloat16)
-        outer = dot(rows[1], kappa_own).astype(jnp.bfloat16)
-        face = dot(rows[2], state_own).astype(jnp.bfloat16)
-        weights[0] = dot(spread[:, 128:256], table(0, 1))
-        weights[1] = dot(outer, table(0, 1))
-        weights[2] = dot(spread[:, 0:256], table(1, 2))
-        weights[3] = dot(spread[:, 128:384], table(3, 2))
-        weights[4] = dot(spread[:, 384:512], table(5, 1))
-        weights[5] = dot(spread[:, 512:640], table(6, 1))
-        weights[6] = dot(face, table(7, 1))
-
-        shape = (BLOCK, EDGE, LANES)
-        x = lax.broadcasted_iota(jnp.int32, shape, 1)
-        lanes = lax.broadcasted_iota(jnp.int32, shape, 2)
-        y, z = lanes // EDGE, lanes % EDGE
+                for i, rows in enumerate(split_pair(values)):
+                    put_rows(staged.at[field, slot], 2 * tile + i - 1, rows)
+
+    def stage_faces(slot):
+        for tile in range(TILES):
+            values = coarse[1, slot, :, tile * 128 : (tile + 1) * 128]
+            for i, rows in enumerate(split_pair(values)):
+                put_rows(outer.at[0], 2 * tile + i, rows)
+                put_rows(outer.at[1], 2 * tile + i - 2, rows)
+        faces[0:SPEC, :] = split_pair(coarse[0, slot, :, 0:128])[0]
+        faces[PITCH : PITCH + SPEC, :] = split_pair(coarse[0, slot, :, COARSE - 128 : COARSE])[1]
+
+    def spread(patch, closed=False):
+        def dot(a, first, count):
+            table = lane_mats[first * 128 : (first + count) * 128, :]
+            return jnp.dot(a, table, preferred_element_type=jnp.float32)
+
+        def keep(index, values, begins):
+            for half in range(2):
+                part = values[:, half * 128 : (half + 1) * 128]
+                for begin in begins:
+                    weights.at[index, half][pl.ds(begin, FLAT, stride=2), :] = part
+
+        z = lane_iota(FLAT) % 8
+
+        def across(field):
+            low, high = staged[field, patch], staged[field, patch + 2]
+            return jnp.where(z == 7, low, jnp.where(z == 0, high, 0.0)).astype(jnp.bfloat16)
+
+        own = staged[1, patch + 1].astype(jnp.bfloat16)
+
+        def beside(values):
+            return jnp.concatenate([own, values], axis=1)
+
+        both = (0, 1)
+        keep(0, dot(own, 8, 1), both)
+        for side in range(2):
+            keep(1, dot(beside(outer[side].astype(jnp.bfloat16)), 0, 2), (side,))
+        if closed:
+            keep(2, dot(own, 2, 1), both)
+        else:
+            keep(2, dot(beside(sides[1].astype(jnp.bfloat16)), 2, 2), both)
+            keep(4, dot(sides[0].astype(jnp.bfloat16), 6, 1), both)
+        keep(3, dot(beside(across(1)), 4, 2), both)
+        keep(5, dot(across(0), 7, 1), both)
+        edge = dot(faces[...].astype(jnp.bfloat16), 8, 1)
+        for half in range(2):
+            face_rows[half] = edge[:, half * 128 : (half + 1) * 128]
+
+    def diffuse(patch, chunk, closed=False):
+        row = lax.broadcasted_iota(jnp.int32, (8, 128), 0)
+        lanes = lax.broadcasted_iota(jnp.int32, (8, 128), 1)
+        odd_x, odd_y, odd_z = row % 2 == 1, (lanes // EDGE) % 2 == 1, lanes % 2 == 1
+        first_x, last_x = row == 0, row == 7
+        first_y, last_y = lanes < EDGE, lanes >= 128 - EDGE
+        face_z = (lanes % EDGE == 0) | (lanes % EDGE == EDGE - 1)
+
+        def one(species):
+            begin = pl.multiple_of(species * EDGE, EDGE)
+            p = [
+                [
+                    cells[patch, species, 8 * h : 8 * h + 8, 128 * v : 128 * v + 128]
+                    for v in range(2)
+                ]
+                for h in range(2)
+            ]
+            down_x = [[pltpu.roll(p[h][v], 1, 0) for v in range(2)] for h in range(2)]
+            up_x = [[pltpu.roll(p[h][v], 7, 0) for v in range(2)] for h in range(2)]
+            down_y = [[pltpu.roll(p[h][v], EDGE, 1) for v in range(2)] for h in range(2)]
+            up_y = [[pltpu.roll(p[h][v], 128 - EDGE, 1) for v in range(2)] for h in range(2)]
+            for h in range(2):
+                for v in range(2):
+                    own = p[h][v]
+
+                    def load(index, h=h, v=v):
+                        return weights[index, v, pl.ds(begin + 8 * h, 8), :]
+
+                    outside = face_rows[v, pl.ds(species + PITCH * h, 1), :]
+                    dx, ux, dy, uy = down_x[h][v], up_x[h][v], down_y[h][v], up_y[h][v]
+                    dz, uz = pltpu.roll(own, 1, 1), pltpu.roll(own, 127, 1)
+                    inner = jnp.where(odd_x, dx, ux) + jnp.where(odd_y, dy, uy)
+                    inner = inner + jnp.where(odd_z, dz, uz)
+                    far_x = jnp.where(odd_x, ux, dx)
+                    far_y = jnp.where(odd_y, uy, dy)
+                    if h == 0:
+                        far_x = jnp.where(first_x, outside, jnp.where(last_x, up_x[1][v], far_x))
+                    else:
+                        far_x = jnp.where(last_x, outside, jnp.where(first_x, down_x[0][v], far_x))
+                    y_outside = own if closed else load(4)
+                    if v == 0:
+                        far_y = jnp.where(first_y, y_outside, jnp.where(last_y, up_y[h][1], far_y))
+                    else:
+                        far_y = jnp.where(last_y, y_outside, jnp.where(first_y, down_y[h][0], far_y))
+                    far_z = jnp.where(face_z, load(5), jnp.where(odd_z, uz, dz))
+                    change = load(0) * (inner - 3.0 * own)
+                    change = change + load(1) * (far_x - own)
+                    change = change + load(2) * (far_y - own)
+                    change = change + load(3) * (far_z - own)
+                    own_ref[patch, species, 8 * h : 8 * h + 8, 128 * v : 128 * v + 128] = own + change
 
         def block(b, carry):
-            species = chunk * CHUNK + b * BLOCK
-            p = cells[patch, pl.ds(species, BLOCK)]
-            at = pl.ds(pl.multiple_of(b * BLOCK * EDGE, BLOCK * EDGE), BLOCK * EDGE)
-            half, half_outer, w_y, w_z, u_y, u_z, u_x = (
-                weights[t, at, :].reshape(shape) for t in range(7)
-            )
-
-            def pair(index, axis, step, extent, outside):
-                up = pltpu.roll(p, extent - step, axis)
-                down = pltpu.roll(p, step, axis)
-                odd = index % 2 == 1
-                inner = jnp.where(odd, down, up)
-                far = jnp.where(odd, up, down)
-                far = jnp.where((index == 0) | (index == EDGE - 1), outside, far)
-                return inner, far
-
-            in_x, out_x = pair(x, 1, 1, EDGE, u_x)
-            in_y, out_y = pair(y, 2, EDGE, LANES, u_y)
-            in_z, out_z = pair(z, 2, 1, LANES, u_z)
-            change = half * (2.0 * (in_x + in_y + in_z) - 6.0 * p)
-            change = change + (half + half_outer) * (out_x - p)
-            change = change + w_y * (out_y - p)
-            change = change + w_z * (out_z - p)
-            own_ref[patch, pl.ds(species, BLOCK)] = p + change
+            for i in range(BLOCK):
+                one(chunk * CHUNK + b * BLOCK + i)
             return carry
 
         lax.fori_loop(0, CHUNK // BLOCK, block, 0)
+
+    lanes8 = lax.broadcasted_iota(jnp.int32, (8, 128), 1)
+    group8 = lax.rem(lanes8 + EDGE, 128) // 32
+
+    def fix(way, patch):
+        low, high = lanes8 < EDGE, lanes8 >= 128 - EDGE
+        packed = None
+        for n in range(2 * CHUNK):
+            species, h, j = n // 2, n % 2, n % 4
+            terms = []
+            for v in range(2):
+                at = slice(species * EDGE + 8 * h, species * EDGE + 8 * h + 8)
+                own = cells[patch, species, 8 * h : 8 * h + 8, 128 * v : 128 * v + 128]
+                terms.append(weights[2, v, at, :] * (weights[4, v, at, :] - own))
+            term = jnp.where(low, terms[0], jnp.where(high, terms[1], 0.0))
+            if j == 0:
+                packed = term
+            else:
+                packed = jnp.where(group8 == j, pltpu.roll(term, 32 * j, 1), packed)
+            if j == 3:
+                fix_out[way, 2 * (n - 3) : 2 * (n - 3) + 8, :] = packed
+
+    def apply_fix(way, source, target, patch):
+        for n in range(2 * CHUNK):
+            species, h, j = n // 2, n % 2, n % 4
+            term = source[way, 2 * (n - j) : 2 * (n - j) + 8, :]
+            if j:
+                term = pltpu.roll(term, 128 - 32 * j, 1)
+            for v in range(2):
+                lanes = slice(128 * v, 128 * v + 128)
+                inside = lanes8 < EDGE if v == 0 else lanes8 >= 128 - EDGE
+                old = target[patch, species, 8 * h : 8 * h + 8, lanes]
+                target[patch, species, 8 * h : 8 * h + 8, lanes] = old + jnp.where(inside, term, 0.0)
 
     def smooth(way, k):
         patch = 5 + k if way == 0 else 4 - k
         slot = (k + 1) // 2
         base = 2 * lax.rem(k + 1, 2) + way
+        stage_faces(patch + 1)
         for field in range(2):
             j = base * 2 + field
             back = 8 * j
@@ -291,29 +361,46 @@
                 low = pltpu.roll(pack_in[0, slot, :, part], back, 1)
                 high = pltpu.roll(pack_in[1, slot, :, part], forth, 1)
                 values = jnp.where(row_of == 7, low, jnp.where(row_of == 0, high, 0.0))
-                stage_tile(tile, values, sides, field)
-        z = lane_iota(DEPTH) % 8
-
-        def across(field):
-            low, high = staged[field, patch], staged[field, patch + 2]
-            return jnp.where(z == 7, low, jnp.where(z == 0, high, 0.0)).astype(jnp.bfloat16)
-
-        state_own = staged[0, patch + 1].astype(jnp.bfloat16)
-        kappa_own = staged[1, patch + 1].astype(jnp.bfloat16)
-        factors = jnp.concatenate(
-            [
-                sides[1].astype(jnp.bfloat16),
-                kappa_own,
-                across(1),
-                sides[0].astype(jnp.bfloat16),
-                across(0),
-            ],
-            axis=1,
-        )
+                for i, rows in enumerate(split_pair(values)):
+                    put_rows(sides.at[field], 2 * tile + i - 1, rows)
+        spread(patch)
+
+        @pl.when(k > 0)
+        def _():
+            load_cells(patch).wait()
+            diffuse(patch, 0)
+            move_copy(way, k, 0).start()
+
+        for chunk in range(1, CHUNKS):
+            diffuse(patch, chunk)
+            move_copy(way, k, chunk).start()
+
+        @pl.when(k == 0)
+        def _():
+            fix(way, patch)
+            fix_copy(way).start()
+
+    for field in range(2):
+        load_coarse(field, 0, *parts[0]).wait()
+    pack(0, (5, 4), 2)
+    pl.semaphore_wait(barrier, 4)
+    for way in range(2):
+        pack_copy(way, 0).start()
+    for slot in (5, 6, 7, 4):
+        stage(slot)
+    load_table().wait()
+    for way, patch in ((0, 5), (1, 4)):
+        stage_faces(patch + 1)
+        spread(patch, closed=True)
         load_cells(patch).wait()
-        for chunk in range(CHUNKS):
-            smooth_chunk(patch, chunk, factors, kappa_own, state_own)
-            move_copy(way, k, chunk).start()
+        diffuse(patch, 0, closed=True)
+        move_copy(way, 0, 0).start()
+    for part in (1, 2):
+        for field in range(2):
+            load_coarse(field, part, *parts[part]).wait()
+    pack(1, (6, 3, 7, 2), 0)
+    for way in range(2):
+        pack_copy(way, 1).start()
 
     def step(k, carry):
         @pl.when(k == 0)
@@ -326,10 +413,17 @@
             for way in range(2):
                 pack_copy(way, 1).wait_recv()
 
+            for way in range(2):
+                move_copy(way, 0, 0).wait_send()
+                apply_fix(way, fix_out, own_ref, 5 - way)
+
         @pl.when(k == 3)
         def _():
             for way in range(2):
                 pack_copy(way, 2).wait_recv()
+                move_copy(way, 0, 0).wait_recv()
+                fix_copy(way).wait_recv()
+                apply_fix(way, fix_in, (left_ref, right_ref)[way], 4 * way)
 
         @pl.when(k == 4)
         def _():
@@ -343,17 +437,16 @@
                     coarse[field, 0, :, part] = low
                     coarse[field, 11, :, part] = high
 
-        stage(7 + k)
-        stage(4 - k)
+        @pl.when(k > 0)
+        def _():
+            stage(7 + k)
+            stage(4 - k)
+
         smooth(0, k)
         smooth(1, k)
 
         @pl.when(k == 0)
         def _():
-            for part in (1, 2):
-                for field in range(2):
-                    load_coarse(field, part, *parts[part]).wait()
-            pack(1, (6, 3, 7, 2), 0)
             pack(2, (8, 1, 9, 0), 0)
             for field in range(2):
                 up = jnp.zeros((SPEC, 128), jnp.float32)
@@ -367,7 +460,6 @@
                 edge_out[0, field] = up
                 edge_out[1, field] = down
             for way in range(2):
-                pack_copy(way, 1).start()
                 pack_copy(way, 2).start()
                 edge_copy(way).start()
 
@@ -380,8 +472,9 @@
             pack_copy(way, slot).wait_send()
         edge_copy(way).wait_send()
         for k in range(HALF):
-            for chunk in range(CHUNKS):
+            for chunk in range(1 if k == 0 else 0, CHUNKS):
                 move_copy(way, k, chunk).wait()
+        fix_copy(way).wait_send()
 
 
 def place_kernel(shift_ref, own_ref, left_ref, right_ref, out_ref, zeros, sem):
@@ -422,43 +515,49 @@
     patch = (SPEC, EDGE, LANES)
     hbm = pl.BlockSpec(memory_space=pltpu.HBM)
     vmem = pl.BlockSpec(memory_space=pltpu.VMEM)
-    row_table = jnp.asarray(row_tables(), bf16)
     lane_table = jnp.asarray(lane_tables(), bf16)
+    operands = (state, coarse_state, coarse_kappa, lane_table)
     own, left, right = pl.pallas_call(
         exchange_kernel,
         name="exchange",
         out_shape=[
             jax.ShapeDtypeStruct((count,) + patch, f32) for count in (PATCHES, HALF, HALF)
         ],
-        in_specs=[hbm] * 5,
+        in_specs=[hbm] * 4,
         out_specs=[vmem] * 3,
         scratch_shapes=[
             pltpu.VMEM((PATCHES,) + patch, f32),
             pltpu.VMEM((2, PATCHES + 2, SPEC, COARSE), f32),
-            pltpu.VMEM(row_table.shape, bf16),
             pltpu.VMEM(lane_table.shape, bf16),
-            pltpu.VMEM((2, PATCHES + 2, DEPTH, 128), f32),
-            pltpu.VMEM((2, DEPTH, 128), f32),
+            pltpu.VMEM((2, PATCHES + 2, FLAT, 128), f32),
+            pltpu.VMEM((2, FLAT, 128), f32),
+            pltpu.VMEM((2, FLAT, 128), f32),
+            pltpu.VMEM((2 * PITCH, 128), f32),
+            pltpu.VMEM((2, 2 * PITCH, 128), f32),
             pltpu.VMEM((2, 3, SPEC, COARSE), f32),
             pltpu.VMEM((2, 3, SPEC, COARSE), f32),
             pltpu.VMEM((2, 2, SPEC, 128), f32),
             pltpu.VMEM((2, 2, SPEC, 128), f32),
-            pltpu.VMEM((7, ROWS, LANES), f32),
+            pltpu.VMEM((6, 2, 2 * FLAT, 128), f32),
+            pltpu.VMEM((2, 4 * CHUNK, 128), f32),
+            pltpu.VMEM((2, 4 * CHUNK, 128), f32),
             pltpu.SemaphoreType.DMA((PATCHES,)),
             pltpu.SemaphoreType.DMA((2, 3)),
-            pltpu.SemaphoreType.DMA((2,)),
+            pltpu.SemaphoreType.DMA,
             pltpu.SemaphoreType.DMA((2, 3)),
             pltpu.SemaphoreType.DMA((2, 3)),
             pltpu.SemaphoreType.DMA((2,)),
             pltpu.SemaphoreType.DMA((2,)),
             pltpu.SemaphoreType.DMA((2, HALF, CHUNKS)),
             pltpu.SemaphoreType.DMA((2, HALF, CHUNKS)),
+            pltpu.SemaphoreType.DMA((2,)),
+            pltpu.SemaphoreType.DMA((2,)),
         ],
         compiler_params=pltpu.CompilerParams(
             collective_id=0, has_side_effects=True, vmem_limit_bytes=36 << 20
         ),
         cost_estimate=pl.CostEstimate(flops=8 << 30, bytes_accessed=12 << 20, transcendentals=0),
-    )(state, coarse_state, coarse_kappa, row_table, lane_table)
+    )(*(pltpu.with_memory_space_constraint(v, pltpu.HBM) for v in operands))
     return pl.pallas_call(
         place_kernel,
         name="place",

time: 67.1 us -> 52.4 us (0.78)
  the two profiles are of different devices: /device:TPU:7 before, /device:TPU:1 now
where the time goes in v2:
time: 52.4 us; the launch traced here: 52.3 us
  Pallas kernels  52.3 us (100%)
    pallas_call x1, Pallas kernels, shards(): pl.pallas_call(exchange_kernel, name='exchange', out_shape=[jax.ShapeDtyp...  49 us
    pallas_call x1, Pallas kernels, shards(): pl.pallas_call(place_kernel, name='place', out_shape=jax.ShapeDtypeStruct...  3.29 us

profile of v2, /device:TPU:1, one launch (start us, length us, event | category | flops | bytes accessed | tf_op | source)
XLA Modules:
  0.0 52.3 jit_solution(8694745673317645098)
XLA Ops:
  0.0 0.0 copy-start
  0.0 49.0 %exchange.1 = (f32[10,20,16,256]{3,2,1,0:T(8,128)S(1)}, f32[5,20,16,256]{3,2,1,0:T(8,128)S(1)}, f32[5,20,16,256]{3,2,1,0:T(8,128)S(1)}) custom-call(f32[10,20,16,256]{3,2,1,0:T(8,128)} %state_ref.1, f32[10,20,640]{2,1,0:T(8,128)} %coarse_state_ref.1, f32[10,20,640]{2,1,0:T(8,128)} %coarse_kappa_ref.1, bf16[1152,256]{1,0:T(8,128)(2,1)} %constant.2.clone.lanes_ref), custom_call_target="tpu_custom_call" | custom-call | flops 8589934592 | bytes 12582912 | tf_op jit(solution)/shard_map/exchange/pallas_call | solution.py:520
  49.0 0.0 copy-done
  49.1 3.3 %place.1 = f32[20,20,16,256]{3,2,1,0:T(8,128)} custom-call(s32[1,32]{1,0:T(1,128)S(1)} %copy-done, f32[10,20,16,256]{3,2,1,0:T(8,128)S(1)} %get-tuple-element.8.own_ref, f32[5,20,16,256]{3,2,1,0:T(8,128)S(1)} %get-tuple-element.9.left_ref, f32[5,20,16,256]{3,2,1,0:T(8,128)S(1)} %get-tuple-element.10.right_ref), custom_call_target="tpu_custom_call" | custom-call | bytes 7340032 | tf_op jit(solution)/shard_map/place/pallas_call | solution.py:561
Async XLA Ops:
  0.0 49.0 %copy-start = (s32[1,32]{1,0:T(1,128)S(1)}, s32[1,32]{1,0:T(1,128)}, u32[]{:S(2)}) copy-start(s32[1,32]{1,0:T(1,128)} %shift_ref.1) | copy-start | bytes 388

commit v3 on v2

--- a/solution.py
+++ b/solution.py
@@ -18,6 +18,7 @@
 CHUNK = 10
 CHUNKS = SPEC // CHUNK
 BLOCK = 2
+EARLY = 2
 FLAT = SPEC * 8
 
 
@@ -74,8 +75,7 @@
     coarse_kappa_ref,
     lanes_ref,
     own_ref,
-    left_ref,
-    right_ref,
+    moved_ref,
     cells,
     coarse,
     lane_mats,
@@ -130,12 +130,12 @@
     for field in range(2):
         load_coarse(field, 0, *parts[0]).start()
     load_table().start()
-    for patch in (5, 4):
+    for patch in (4, 5):
         load_cells(patch).start()
     for part in (1, 2):
         for field in range(2):
             load_coarse(field, part, *parts[part]).start()
-    for patch in (6, 3, 7, 2, 8, 1, 9, 0):
+    for patch in (3, 6, 2, 7, 1, 8, 0, 9):
         load_cells(patch).start()
 
     barrier = pltpu.get_barrier_semaphore()
@@ -170,6 +170,12 @@
             device_id_type=MESH,
         )
 
+    def toward(way):
+        return (jnp.where(way == 0, ahead[0], behind[0]), group)
+
+    def leaving(way, k):
+        return jnp.where(way == 0, HALF + k, HALF - 1 - k)
+
     def edge_copy(way):
         return pltpu.make_async_remote_copy(
             src_ref=edge_out.at[way],
@@ -181,17 +187,26 @@
         )
 
     def move_copy(way, k, chunk):
-        patch = 5 + k if way == 0 else 4 - k
-        slot = k if way == 0 else 4 - k
         part = pl.ds(chunk * CHUNK, CHUNK)
         return pltpu.make_async_remote_copy(
-            src_ref=own_ref.at[patch, part],
-            dst_ref=(left_ref, right_ref)[way].at[slot, part],
+            src_ref=own_ref.at[leaving(way, k), part],
+            dst_ref=moved_ref.at[way, jnp.where(way == 0, k, HALF - 1 - k), part],
             send_sem=move_send.at[way, k, chunk],
             recv_sem=move_recv.at[way, k, chunk],
-            device_id=(ahead, behind)[way],
+            device_id=toward(way),
             device_id_type=MESH,
         )
+
+    def sends(way):
+        return jnp.where(way == 0, curve < n_curve - 1, curve > 0)
+
+    def gets(way):
+        return jnp.where(way == 0, curve > 0, curve < n_curve - 1)
+
+    def send_move(way, k, chunk):
+        @pl.when(sends(way))
+        def _():
+            move_copy(way, k, chunk).start()
 
     def fix_copy(way):
         return pltpu.make_async_remote_copy(
@@ -199,7 +214,7 @@
             dst_ref=fix_in.at[way],
             send_sem=fix_send.at[way],
             recv_sem=fix_recv.at[way],
-            device_id=(ahead, behind)[way],
+            device_id=toward(way),
             device_id_type=MESH,
         )
 
@@ -219,17 +234,17 @@
         faces[0:SPEC, :] = split_pair(coarse[0, slot, :, 0:128])[0]
         faces[PITCH : PITCH + SPEC, :] = split_pair(coarse[0, slot, :, COARSE - 128 : COARSE])[1]
 
-    def spread(patch, closed=False):
-        def dot(a, first, count):
-            table = lane_mats[first * 128 : (first + count) * 128, :]
-            return jnp.dot(a, table, preferred_element_type=jnp.float32)
-
-        def keep(index, values, begins):
-            for half in range(2):
-                part = values[:, half * 128 : (half + 1) * 128]
-                for begin in begins:
-                    weights.at[index, half][pl.ds(begin, FLAT, stride=2), :] = part
-
+    def dot(a, first, count):
+        table = lane_mats[first * 128 : (first + count) * 128, :]
+        return jnp.dot(a, table, preferred_element_type=jnp.float32)
+
+    def keep(way, index, values, begins=(0, 1)):
+        for half in range(2):
+            part = values[:, half * 128 : (half + 1) * 128]
+            for begin in begins:
+                weights.at[way, index, half][pl.ds(begin, FLAT, stride=2), :] = part
+
+    def spread(way, patch):
         z = lane_iota(FLAT) % 8
 
         def across(field):
@@ -241,22 +256,25 @@
         def beside(values):
             return jnp.concatenate([own, values], axis=1)
 
-        both = (0, 1)
-        keep(0, dot(own, 8, 1), both)
+        keep(way, 0, dot(own, 8, 1))
         for side in range(2):
-            keep(1, dot(beside(outer[side].astype(jnp.bfloat16)), 0, 2), (side,))
-        if closed:
-            keep(2, dot(own, 2, 1), both)
-        else:
-            keep(2, dot(beside(sides[1].astype(jnp.bfloat16)), 2, 2), both)
-            keep(4, dot(sides[0].astype(jnp.bfloat16), 6, 1), both)
-        keep(3, dot(beside(across(1)), 4, 2), both)
-        keep(5, dot(across(0), 7, 1), both)
+            keep(way, 1, dot(beside(outer[side].astype(jnp.bfloat16)), 0, 2), (side,))
+        keep(way, 3, dot(beside(across(1)), 4, 2))
+        keep(way, 5, dot(across(0), 7, 1))
         edge = dot(faces[...].astype(jnp.bfloat16), 8, 1)
         for half in range(2):
-            face_rows[half] = edge[:, half * 128 : (half + 1) * 128]
-
-    def diffuse(patch, chunk, closed=False):
+            face_rows[way, half] = edge[:, half * 128 : (half + 1) * 128]
+
+    def spread_y(way, patch, closed):
+        own = staged[1, patch + 1].astype(jnp.bfloat16)
+        if closed:
+            keep(way, 2, dot(own, 2, 1))
+        else:
+            beside = jnp.concatenate([own, sides[1].astype(jnp.bfloat16)], axis=1)
+            keep(way, 2, dot(beside, 2, 2))
+            keep(way, 4, dot(sides[0].astype(jnp.bfloat16), 6, 1))
+
+    def diffuse(way, patch, chunk, closed=False):
         row = lax.broadcasted_iota(jnp.int32, (8, 128), 0)
         lanes = lax.broadcasted_iota(jnp.int32, (8, 128), 1)
         odd_x, odd_y, odd_z = row % 2 == 1, (lanes // EDGE) % 2 == 1, lanes % 2 == 1
@@ -282,9 +300,9 @@
                     own = p[h][v]
 
                     def load(index, h=h, v=v):
-                        return weights[index, v, pl.ds(begin + 8 * h, 8), :]
-
-                    outside = face_rows[v, pl.ds(species + PITCH * h, 1), :]
+                        return weights[way, index, v, pl.ds(begin + 8 * h, 8), :]
+
+                    outside = face_rows[way, v, pl.ds(species + PITCH * h, 1), :]
                     dx, ux, dy, uy = down_x[h][v], up_x[h][v], down_y[h][v], up_y[h][v]
                     dz, uz = pltpu.roll(own, 1, 1), pltpu.roll(own, 127, 1)
                     inner = jnp.where(odd_x, dx, ux) + jnp.where(odd_y, dy, uy)
@@ -320,13 +338,13 @@
     def fix(way, patch):
         low, high = lanes8 < EDGE, lanes8 >= 128 - EDGE
         packed = None
-        for n in range(2 * CHUNK):
+        for n in range(2 * EARLY * CHUNK):
             species, h, j = n // 2, n % 2, n % 4
             terms = []
             for v in range(2):
                 at = slice(species * EDGE + 8 * h, species * EDGE + 8 * h + 8)
                 own = cells[patch, species, 8 * h : 8 * h + 8, 128 * v : 128 * v + 128]
-                terms.append(weights[2, v, at, :] * (weights[4, v, at, :] - own))
+                terms.append(weights[way, 2, v, at, :] * (weights[way, 4, v, at, :] - own))
             term = jnp.where(low, terms[0], jnp.where(high, terms[1], 0.0))
             if j == 0:
                 packed = term
@@ -336,7 +354,7 @@
                 fix_out[way, 2 * (n - 3) : 2 * (n - 3) + 8, :] = packed
 
     def apply_fix(way, source, target, patch):
-        for n in range(2 * CHUNK):
+        for n in range(2 * EARLY * CHUNK):
             species, h, j = n // 2, n % 2, n % 4
             term = source[way, 2 * (n - j) : 2 * (n - j) + 8, :]
             if j:
@@ -348,10 +366,15 @@
                 target[patch, species, 8 * h : 8 * h + 8, lanes] = old + jnp.where(inside, term, 0.0)
 
     def smooth(way, k):
-        patch = 5 + k if way == 0 else 4 - k
+        patch = leaving(way, k)
         slot = (k + 1) // 2
         base = 2 * lax.rem(k + 1, 2) + way
-        stage_faces(patch + 1)
+
+        @pl.when(k > 0)
+        def _():
+            stage_faces(patch + 1)
+            spread(way, patch)
+
         for field in range(2):
             j = base * 2 + field
             back = 8 * j
@@ -363,38 +386,47 @@
                 values = jnp.where(row_of == 7, low, jnp.where(row_of == 0, high, 0.0))
                 for i, rows in enumerate(split_pair(values)):
                     put_rows(sides.at[field], 2 * tile + i - 1, rows)
-        spread(patch)
+        spread_y(way, patch, False)
 
         @pl.when(k > 0)
         def _():
             load_cells(patch).wait()
-            diffuse(patch, 0)
-            move_copy(way, k, 0).start()
-
-        for chunk in range(1, CHUNKS):
-            diffuse(patch, chunk)
-            move_copy(way, k, chunk).start()
+            for chunk in range(EARLY):
+                diffuse(way, patch, chunk)
+                send_move(way, k, chunk)
+
+        for chunk in range(EARLY, CHUNKS):
+            diffuse(way, patch, chunk)
+            send_move(way, k, chunk)
 
         @pl.when(k == 0)
         def _():
             fix(way, patch)
-            fix_copy(way).start()
+
+            @pl.when(sends(way))
+            def _():
+                fix_copy(way).start()
 
     for field in range(2):
         load_coarse(field, 0, *parts[0]).wait()
-    pack(0, (5, 4), 2)
-    pl.semaphore_wait(barrier, 4)
-    for way in range(2):
-        pack_copy(way, 0).start()
     for slot in (5, 6, 7, 4):
         stage(slot)
     load_table().wait()
-    for way, patch in ((0, 5), (1, 4)):
+    for turn in range(2):
+        way = 1 - turn
+        patch = leaving(way, 0)
         stage_faces(patch + 1)
-        spread(patch, closed=True)
+        spread(way, patch)
+        spread_y(way, patch, True)
         load_cells(patch).wait()
-        diffuse(patch, 0, closed=True)
-        move_copy(way, 0, 0).start()
+        diffuse(way, patch, 0, closed=True)
+        if turn == 0:
+            pl.semaphore_wait(barrier, 4)
+        send_move(way, 0, 0)
+        if turn == 0:
+            pack(0, (5, 4), 2)
+            for side in range(2):
+                pack_copy(side, 0).start()
     for part in (1, 2):
         for field in range(2):
             load_coarse(field, part, *parts[part]).wait()
@@ -402,30 +434,40 @@
     for way in range(2):
         pack_copy(way, 1).start()
 
-    def step(k, carry):
-        @pl.when(k == 0)
+    for chunk in range(1, EARLY):
+        for turn in range(2):
+            way = 1 - turn
+            diffuse(way, leaving(way, 0), chunk, closed=True)
+            send_move(way, 0, chunk)
+
+    def step(m, carry):
+        k = m // 2
+        for slot, turn in ((0, 0), (1, 2), (2, 6)):
+
+            @pl.when(m == turn)
+            def _(slot=slot):
+                for way in range(2):
+                    pack_copy(way, slot).wait_recv()
+
+        @pl.when(m == 6)
         def _():
             for way in range(2):
-                pack_copy(way, 0).wait_recv()
-
-        @pl.when(k == 1)
-        def _():
-            for way in range(2):
-                pack_copy(way, 1).wait_recv()
-
-            for way in range(2):
-                move_copy(way, 0, 0).wait_send()
+
+                @pl.when(sends(way))
+                def _(way=way):
+                    for chunk in range(EARLY):
+                        move_copy(way, 0, chunk).wait_send()
+
                 apply_fix(way, fix_out, own_ref, 5 - way)
 
-        @pl.when(k == 3)
-        def _():
-            for way in range(2):
-                pack_copy(way, 2).wait_recv()
-                move_copy(way, 0, 0).wait_recv()
-                fix_copy(way).wait_recv()
-                apply_fix(way, fix_in, (left_ref, right_ref)[way], 4 * way)
-
-        @pl.when(k == 4)
+                @pl.when(gets(way))
+                def _(way=way):
+                    for chunk in range(EARLY):
+                        move_copy(way, 0, chunk).wait_recv()
+                    fix_copy(way).wait_recv()
+                    apply_fix(way, fix_in, moved_ref.at[way], 4 * way)
+
+        @pl.when(m == 8)
         def _():
             for way in range(2):
                 edge_copy(way).wait_recv()
@@ -437,15 +479,14 @@
                     coarse[field, 0, :, part] = low
                     coarse[field, 11, :, part] = high
 
-        @pl.when(k > 0)
+        @pl.when((m > 1) & (lax.rem(m, 2) == 0))
         def _():
             stage(7 + k)
             stage(4 - k)
 
-        smooth(0, k)
-        smooth(1, k)
-
-        @pl.when(k == 0)
+        smooth(1 - lax.rem(m, 2), k)
+
+        @pl.when(m == 1)
         def _():
             pack(2, (8, 1, 9, 0), 0)
             for field in range(2):
@@ -465,19 +506,28 @@
 
         return carry
 
-    lax.fori_loop(0, HALF, step, 0)
+    lax.fori_loop(0, 2 * HALF, step, 0)
 
     for way in range(2):
         for slot in range(3):
             pack_copy(way, slot).wait_send()
         edge_copy(way).wait_send()
-        for k in range(HALF):
-            for chunk in range(1 if k == 0 else 0, CHUNKS):
-                move_copy(way, k, chunk).wait()
-        fix_copy(way).wait_send()
-
-
-def place_kernel(shift_ref, own_ref, left_ref, right_ref, out_ref, zeros, sem):
+
+        @pl.when(sends(way))
+        def _(way=way):
+            fix_copy(way).wait_send()
+            for k in range(HALF):
+                for chunk in range(EARLY if k == 0 else 0, CHUNKS):
+                    move_copy(way, k, chunk).wait_send()
+
+        @pl.when(gets(way))
+        def _(way=way):
+            for k in range(HALF):
+                for chunk in range(EARLY if k == 0 else 0, CHUNKS):
+                    move_copy(way, k, chunk).wait_recv()
+
+
+def place_kernel(shift_ref, own_ref, moved_ref, out_ref, zeros, sem):
     curve = lax.axis_index("curve")
     here = shift_ref[0, curve]
     before = jnp.where(curve > 0, shift_ref[0, jnp.maximum(curve - 1, 0)], 0)
@@ -493,11 +543,11 @@
 
         @pl.when(used & (position < 0))
         def _():
-            put(left_ref.at[jnp.clip(position + HALF, 0, HALF - 1)])
+            put(moved_ref.at[0, jnp.clip(position + HALF, 0, HALF - 1)])
 
         @pl.when(used & (position >= PATCHES))
         def _():
-            put(right_ref.at[jnp.clip(position - PATCHES, 0, HALF - 1)])
+            put(moved_ref.at[1, jnp.clip(position - PATCHES, 0, HALF - 1)])
 
         @pl.when(used & (position >= 0) & (position < PATCHES))
         def _():
@@ -517,14 +567,15 @@
     vmem = pl.BlockSpec(memory_space=pltpu.VMEM)
     lane_table = jnp.asarray(lane_tables(), bf16)
     operands = (state, coarse_state, coarse_kappa, lane_table)
-    own, left, right = pl.pallas_call(
+    own, moved = pl.pallas_call(
         exchange_kernel,
         name="exchange",
         out_shape=[
-            jax.ShapeDtypeStruct((count,) + patch, f32) for count in (PATCHES, HALF, HALF)
+            jax.ShapeDtypeStruct((PATCHES,) + patch, f32),
+            jax.ShapeDtypeStruct((2, HALF) + patch, f32),
         ],
         in_specs=[hbm] * 4,
-        out_specs=[vmem] * 3,
+        out_specs=[vmem] * 2,
         scratch_shapes=[
             pltpu.VMEM((PATCHES,) + patch, f32),
             pltpu.VMEM((2, PATCHES + 2, SPEC, COARSE), f32),
@@ -533,14 +584,14 @@
             pltpu.VMEM((2, FLAT, 128), f32),
             pltpu.VMEM((2, FLAT, 128), f32),
             pltpu.VMEM((2 * PITCH, 128), f32),
-            pltpu.VMEM((2, 2 * PITCH, 128), f32),
+            pltpu.VMEM((2, 2, 2 * PITCH, 128), f32),
             pltpu.VMEM((2, 3, SPEC, COARSE), f32),
             pltpu.VMEM((2, 3, SPEC, COARSE), f32),
             pltpu.VMEM((2, 2, SPEC, 128), f32),
             pltpu.VMEM((2, 2, SPEC, 128), f32),
-            pltpu.VMEM((6, 2, 2 * FLAT, 128), f32),
-            pltpu.VMEM((2, 4 * CHUNK, 128), f32),
-            pltpu.VMEM((2, 4 * CHUNK, 128), f32),
+            pltpu.VMEM((2, 6, 2, 2 * FLAT, 128), f32),
+            pltpu.VMEM((2, 4 * EARLY * CHUNK, 128), f32),
+            pltpu.VMEM((2, 4 * EARLY * CHUNK, 128), f32),
             pltpu.SemaphoreType.DMA((PATCHES,)),
             pltpu.SemaphoreType.DMA((2, 3)),
             pltpu.SemaphoreType.DMA,
@@ -562,12 +613,12 @@
         place_kernel,
         name="place",
         out_shape=jax.ShapeDtypeStruct((2 * PATCHES,) + patch, f32),
-        in_specs=[pl.BlockSpec(memory_space=pltpu.SMEM)] + [vmem] * 3,
+        in_specs=[pl.BlockSpec(memory_space=pltpu.SMEM)] + [vmem] * 2,
         out_specs=hbm,
         scratch_shapes=[pltpu.VMEM(patch, f32), pltpu.SemaphoreType.DMA],
         compiler_params=pltpu.CompilerParams(vmem_limit_bytes=16 << 20),
         cost_estimate=pl.CostEstimate(flops=0, bytes_accessed=7 << 20, transcendentals=0),
-    )(bound_shift, own, left, right)
+    )(bound_shift, own, moved)
 
 
 def solution(mesh):

time: 52.4 us -> 50.9 us (0.971)
  Pallas kernels: 52.3 us -> 50.5 us
    pallas_call x1, Pallas kernels: 49 us -> 47.2 us  [shards(): pl.pallas_call(exchange_kernel, name='exchange', out_shape=[jax.ShapeDtyp...]
where the time goes in v3:
time: 50.9 us; the launch traced here: 50.5 us
  Pallas kernels  50.5 us (99%)
    pallas_call x1, Pallas kernels, shards(): pl.pallas_call(exchange_kernel, name='exchange', out_shape=[jax.ShapeDtyp...  47.2 us
    pallas_call x1, Pallas kernels, shards(): pl.pallas_call(place_kernel, name='place', out_shape=jax.ShapeDtypeStruct...  3.29 us

profile of v3, /device:TPU:1, one launch (start us, length us, event | category | flops | bytes accessed | tf_op | source)
XLA Modules:
  0.0 50.5 jit_solution(12439566438346261997)
XLA Ops:
  0.0 0.0 copy-start
  0.0 47.2 %exchange.1 = (f32[10,20,16,256]{3,2,1,0:T(8,128)S(1)}, f32[2,5,20,16,256]{4,3,2,1,0:T(8,128)S(1)}) custom-call(f32[10,20,16,256]{3,2,1,0:T(8,128)} %state_ref.1, f32[10,20,640]{2,1,0:T(8,128)} %coarse_state_ref.1, f32[10,20,640]{2,1,0:T(8,128)} %coarse_kappa_ref.1, bf16[1152,256]{1,0:T(8,128)(2,1)} %constant.2.clone.lanes_ref), custom_call_target="tpu_custom_call" | custom-call | flops 8589934592 | bytes 12582912 | tf_op jit(solution)/shard_map/exchange/pallas_call | solution.py:570
  47.2 0.0 copy-done
  47.3 3.3 %place.1 = f32[20,20,16,256]{3,2,1,0:T(8,128)} custom-call(s32[1,32]{1,0:T(1,128)S(1)} %copy-done, f32[10,20,16,256]{3,2,1,0:T(8,128)S(1)} %get-tuple-element.7.own_ref, f32[2,5,20,16,256]{4,3,2,1,0:T(8,128)S(1)} %get-tuple-element.8.moved_ref), custom_call_target="tpu_custom_call" | custom-call | bytes 7340032 | tf_op jit(solution)/shard_map/place/pallas_call | solution.py:612
Async XLA Ops:
  0.0 47.2 %copy-start = (s32[1,32]{1,0:T(1,128)S(1)}, s32[1,32]{1,0:T(1,128)}, u32[]{:S(2)}) copy-start(s32[1,32]{1,0:T(1,128)} %shift_ref.1) | copy-start | bytes 388

commit v4 on v3

--- a/solution.py
+++ b/solution.py
@@ -107,6 +107,7 @@
     group = lax.axis_index("group")
     n_curve = lax.axis_size("curve")
     n_group = lax.axis_size("group")
+    core = lax.rem(group, 2)
     ahead = (lax.rem(curve + 1, n_curve), group)
     behind = (lax.rem(curve + n_curve - 1, n_curve), group)
     above = (curve, lax.rem(group + 1, n_group))
@@ -420,25 +421,31 @@
         spread_y(way, patch, True)
         load_cells(patch).wait()
         diffuse(way, patch, 0, closed=True)
-        if turn == 0:
-            pl.semaphore_wait(barrier, 4)
-        send_move(way, 0, 0)
-        if turn == 0:
-            pack(0, (5, 4), 2)
-            for side in range(2):
-                pack_copy(side, 0).start()
+    pack(0, (5, 4), 2)
+    pl.semaphore_wait(barrier, 4)
+    send_move(1, 0, 0)
+    for side in range(2):
+        pack_copy(side, 0).start()
+    send_move(0, 0, 0)
     for part in (1, 2):
         for field in range(2):
             load_coarse(field, part, *parts[part]).wait()
     pack(1, (6, 3, 7, 2), 0)
-    for way in range(2):
-        pack_copy(way, 1).start()
-
+
+    def send_packs(when, slot):
+        @pl.when(when)
+        def _():
+            for side in range(2):
+                pack_copy(side, slot).start()
+
+    send_packs(core == 0, 1)
     for chunk in range(1, EARLY):
         for turn in range(2):
             way = 1 - turn
             diffuse(way, leaving(way, 0), chunk, closed=True)
             send_move(way, 0, chunk)
+            if chunk + turn == 1:
+                send_packs(core == 1, 1)
 
     def step(m, carry):
         k = m // 2
@@ -474,10 +481,10 @@
             for field in range(2):
                 for tile in range(TILES):
                     part = slice(tile * 128, (tile + 1) * 128)
-                    low = pltpu.roll(edge_in[0, field], (7 - tile) % 128, 1)
-                    high = pltpu.roll(edge_in[1, field], (128 - tile) % 128, 1)
-                    coarse[field, 0, :, part] = low
-                    coarse[field, 11, :, part] = high
+                    places = [4 * field + max(tile - 1, 0), 4 * field + min(tile, 3)]
+                    for side, slot, begin in ((0, 0, 71), (1, PATCHES + 1, 64)):
+                        low, high = (pltpu.roll(edge_in[side], begin - place, 1) for place in places)
+                        coarse[field, slot, :, part] = jnp.where(lane < 64, low, high)
 
         @pl.when((m > 1) & (lax.rem(m, 2) == 0))
         def _():
@@ -489,21 +496,26 @@
         @pl.when(m == 1)
         def _():
             pack(2, (8, 1, 9, 0), 0)
-            for field in range(2):
-                up = jnp.zeros((SPEC, 128), jnp.float32)
-                down = jnp.zeros((SPEC, 128), jnp.float32)
-                for tile in range(TILES):
-                    part = slice(tile * 128, (tile + 1) * 128)
-                    last = coarse[field, PATCHES, :, part]
-                    first = coarse[field, 1, :, part]
-                    up = jnp.where(lane % 8 == tile, pltpu.roll(last, (128 + tile - 7) % 128, 1), up)
-                    down = jnp.where(lane % 8 == tile, pltpu.roll(first, tile, 1), down)
-                edge_out[0, field] = up
-                edge_out[1, field] = down
+            up = jnp.zeros((SPEC, 128), jnp.float32)
+            down = jnp.zeros((SPEC, 128), jnp.float32)
+            for place in range(8):
+                field, tile = place // 4, place % 4
+
+                def halves(patch, shift, field=field, tile=tile):
+                    low, high = (
+                        coarse[field, patch + 1, :, t * 128 : (t + 1) * 128] for t in (tile, tile + 1)
+                    )
+                    return jnp.where(lane < 64, pltpu.roll(low, shift, 1), pltpu.roll(high, shift, 1))
+
+                here = lane % 8 == place
+                up = jnp.where(here, halves(PATCHES - 1, 57 + place), up)
+                down = jnp.where(here, halves(0, 64 + place), down)
+            edge_out[0] = up
+            edge_out[1] = down
             for way in range(2):
-                pack_copy(way, 2).start()
                 edge_copy(way).start()
 
+        send_packs(m == 1 + core, 2)
         return carry
 
     lax.fori_loop(0, 2 * HALF, step, 0)
@@ -587,8 +599,8 @@
             pltpu.VMEM((2, 2, 2 * PITCH, 128), f32),
             pltpu.VMEM((2, 3, SPEC, COARSE), f32),
             pltpu.VMEM((2, 3, SPEC, COARSE), f32),
-            pltpu.VMEM((2, 2, SPEC, 128), f32),
-            pltpu.VMEM((2, 2, SPEC, 128), f32),
+            pltpu.VMEM((2, SPEC, 128), f32),
+            pltpu.VMEM((2, SPEC, 128), f32),
             pltpu.VMEM((2, 6, 2, 2 * FLAT, 128), f32),
             pltpu.VMEM((2, 4 * EARLY * CHUNK, 128), f32),
             pltpu.VMEM((2, 4 * EARLY * CHUNK, 128), f32),

time: 50.9 us -> 50.4 us (level)
  Pallas kernels: 50.5 us -> 49.8 us
    pallas_call x1, Pallas kernels: 47.2 us -> 46.5 us  [shards(): pl.pallas_call(exchange_kernel, name='exchange', out_shape=[jax.ShapeDtyp...]
where the time goes in v4:
time: 50.4 us; the launch traced here: 49.8 us
  Pallas kernels  49.8 us (99%)
    pallas_call x1, Pallas kernels, shards(): pl.pallas_call(exchange_kernel, name='exchange', out_shape=[jax.ShapeDtyp...  46.5 us
    pallas_call x1, Pallas kernels, shards(): pl.pallas_call(place_kernel, name='place', out_shape=jax.ShapeDtypeStruct...  3.29 us

profile of v4, /device:TPU:1, one launch (start us, length us, event | category | flops | bytes accessed | tf_op | source)
XLA Modules:
  0.0 49.8 jit_solution(7431993263091073707)
XLA Ops:
  0.0 0.0 copy-start
  0.0 46.5 %exchange.1 = (f32[10,20,16,256]{3,2,1,0:T(8,128)S(1)}, f32[2,5,20,16,256]{4,3,2,1,0:T(8,128)S(1)}) custom-call(f32[10,20,16,256]{3,2,1,0:T(8,128)} %state_ref.1, f32[10,20,640]{2,1,0:T(8,128)} %coarse_state_ref.1, f32[10,20,640]{2,1,0:T(8,128)} %coarse_kappa_ref.1, bf16[1152,256]{1,0:T(8,128)(2,1)} %constant.2.clone.lanes_ref), custom_call_target="tpu_custom_call" | custom-call | flops 8589934592 | bytes 12582912 | tf_op jit(solution)/shard_map/exchange/pallas_call | solution.py:582
  46.5 0.0 copy-done
  46.5 3.3 %place.1 = f32[20,20,16,256]{3,2,1,0:T(8,128)} custom-call(s32[1,32]{1,0:T(1,128)S(1)} %copy-done, f32[10,20,16,256]{3,2,1,0:T(8,128)S(1)} %get-tuple-element.7.own_ref, f32[2,5,20,16,256]{4,3,2,1,0:T(8,128)S(1)} %get-tuple-element.8.moved_ref), custom_call_target="tpu_custom_call" | custom-call | bytes 7340032 | tf_op jit(solution)/shard_map/place/pallas_call | solution.py:624
Async XLA Ops:
  0.0 46.5 %copy-start = (s32[1,32]{1,0:T(1,128)S(1)}, s32[1,32]{1,0:T(1,128)}, u32[]{:S(2)}) copy-start(s32[1,32]{1,0:T(1,128)} %shift_ref.1) | copy-start | bytes 388

commit v5 on v4

--- a/solution.py
+++ b/solution.py
@@ -20,6 +20,7 @@
 BLOCK = 2
 EARLY = 2
 FLAT = SPEC * 8
+ROOM = PITCH * 8
 
 
 def lane_tables():
@@ -249,17 +250,17 @@
         z = lane_iota(FLAT) % 8
 
         def across(field):
-            low, high = staged[field, patch], staged[field, patch + 2]
+            low, high = staged[field, patch, 0:FLAT], staged[field, patch + 2, 0:FLAT]
             return jnp.where(z == 7, low, jnp.where(z == 0, high, 0.0)).astype(jnp.bfloat16)
 
-        own = staged[1, patch + 1].astype(jnp.bfloat16)
+        own = staged[1, patch + 1, 0:FLAT].astype(jnp.bfloat16)
 
         def beside(values):
             return jnp.concatenate([own, values], axis=1)
 
         keep(way, 0, dot(own, 8, 1))
         for side in range(2):
-            keep(way, 1, dot(beside(outer[side].astype(jnp.bfloat16)), 0, 2), (side,))
+            keep(way, 1, dot(beside(outer[side, 0:FLAT].astype(jnp.bfloat16)), 0, 2), (side,))
         keep(way, 3, dot(beside(across(1)), 4, 2))
         keep(way, 5, dot(across(0), 7, 1))
         edge = dot(faces[...].astype(jnp.bfloat16), 8, 1)
@@ -267,13 +268,13 @@
             face_rows[way, half] = edge[:, half * 128 : (half + 1) * 128]
 
     def spread_y(way, patch, closed):
-        own = staged[1, patch + 1].astype(jnp.bfloat16)
+        own = staged[1, patch + 1, 0:FLAT].astype(jnp.bfloat16)
         if closed:
             keep(way, 2, dot(own, 2, 1))
         else:
-            beside = jnp.concatenate([own, sides[1].astype(jnp.bfloat16)], axis=1)
+            beside = jnp.concatenate([own, sides[1, 0:FLAT].astype(jnp.bfloat16)], axis=1)
             keep(way, 2, dot(beside, 2, 2))
-            keep(way, 4, dot(sides[0].astype(jnp.bfloat16), 6, 1))
+            keep(way, 4, dot(sides[0, 0:FLAT].astype(jnp.bfloat16), 6, 1))
 
     def diffuse(way, patch, chunk, closed=False):
         row = lax.broadcasted_iota(jnp.int32, (8, 128), 0)
@@ -592,9 +593,9 @@
             pltpu.VMEM((PATCHES,) + patch, f32),
             pltpu.VMEM((2, PATCHES + 2, SPEC, COARSE), f32),
             pltpu.VMEM(lane_table.shape, bf16),
-            pltpu.VMEM((2, PATCHES + 2, FLAT, 128), f32),
-            pltpu.VMEM((2, FLAT, 128), f32),
-            pltpu.VMEM((2, FLAT, 128), f32),
+            pltpu.VMEM((2, PATCHES + 2, ROOM, 128), f32),
+            pltpu.VMEM((2, ROOM, 128), f32),
+            pltpu.VMEM((2, ROOM, 128), f32),
             pltpu.VMEM((2 * PITCH, 128), f32),
             pltpu.VMEM((2, 2, 2 * PITCH, 128), f32),
             pltpu.VMEM((2, 3, SPEC, COARSE), f32),

time: 50.4 us -> 50.4 us (level)
  no operation moved by 1% of the time
where the time goes in v5:
time: 50.4 us; the launch traced here: 49.8 us
  Pallas kernels  49.8 us (99%)
    pallas_call x1, Pallas kernels, shards(): pl.pallas_call(exchange_kernel, name='exchange', out_shape=[jax.ShapeDtyp...  46.5 us
    pallas_call x1, Pallas kernels, shards(): pl.pallas_call(place_kernel, name='place', out_shape=jax.ShapeDtypeStruct...  3.29 us

profile of v5, /device:TPU:1, one launch (start us, length us, event | category | flops | bytes accessed | tf_op | source)
XLA Modules:
  0.0 49.8 jit_solution(6161687621438608823)
XLA Ops:
  0.0 0.0 copy-start
  0.0 46.5 %exchange.1 = (f32[10,20,16,256]{3,2,1,0:T(8,128)S(1)}, f32[2,5,20,16,256]{4,3,2,1,0:T(8,128)S(1)}) custom-call(f32[10,20,16,256]{3,2,1,0:T(8,128)} %state_ref.1, f32[10,20,640]{2,1,0:T(8,128)} %coarse_state_ref.1, f32[10,20,640]{2,1,0:T(8,128)} %coarse_kappa_ref.1, bf16[1152,256]{1,0:T(8,128)(2,1)} %constant.2.clone.lanes_ref), custom_call_target="tpu_custom_call" | custom-call | flops 8589934592 | bytes 12582912 | tf_op jit(solution)/shard_map/exchange/pallas_call | solution.py:583
  46.5 0.0 copy-done
  46.5 3.3 %place.1 = f32[20,20,16,256]{3,2,1,0:T(8,128)} custom-call(s32[1,32]{1,0:T(1,128)S(1)} %copy-done, f32[10,20,16,256]{3,2,1,0:T(8,128)S(1)} %get-tuple-element.7.own_ref, f32[2,5,20,16,256]{4,3,2,1,0:T(8,128)S(1)} %get-tuple-element.8.moved_ref), custom_call_target="tpu_custom_call" | custom-call | bytes 7340032 | tf_op jit(solution)/shard_map/place/pallas_call | solution.py:625
Async XLA Ops:
  0.0 46.5 %copy-start = (s32[1,32]{1,0:T(1,128)S(1)}, s32[1,32]{1,0:T(1,128)}, u32[]{:S(2)}) copy-start(s32[1,32]{1,0:T(1,128)} %shift_ref.1) | copy-start | bytes 388
